TPU v7x, 512 devices: a whole 4x8x8 slice. The times are simulated.
512 devices in a mesh: lon: 32 (over x, z_hi, core), lat: 16 (over y, z_lo).
Axes of the slice: x: 4, y: 8, z: 8 (z_hi: 4, z_lo: 2; z = z_hi * 2 + z_lo), core: 2. Of those that a mesh axis runs over, the one named last changes fastest.
Arguments:
- fields: bfloat16 [1, 64, 256, 4096], P(None, None, 'lat', 'lon'), may hold values from -6 to 6
- cotangent: bfloat16 [1, 64, 256, 4096], P(None, None, 'lat', 'lon'), may hold values from -6 to 6
- ocean_mask: int32 [256, 4096], P('lat', 'lon'), may hold values 0 or 1
- seam_partner: int32 [4096], replicated, may hold values from 0 to 4095, as said below
- depth_weight: bfloat16 [64, 7, 7], replicated, may hold values from -0.875 to 0.875
- norm_gain: bfloat16 [64], replicated, may hold values from 0.5 to 1.5
- layer_norm_bias: bfloat16 [64], replicated, may hold values from -3 to 3
- up_weight: bfloat16 [256, 64], replicated, may hold values from -0.75 to 0.75
- up_bias: bfloat16 [256], replicated, may hold values from -3 to 3
- down_weight: bfloat16 [64, 256], replicated, may hold values from -0.375 to 0.375
- layer_scale: bfloat16 [64], replicated, may hold values from 0.5 to 1.5
Outputs:
- output: bfloat16 [1, 64, 256, 4096], P(None, None, 'lat', 'lon')
- grad_fields: bfloat16 [1, 64, 256, 4096], P(None, None, 'lat', 'lon')
- grad_depth: float32 [64, 7, 7], replicated
- grad_gain: float32 [64], replicated
- grad_bias: float32 [64], replicated
- grad_up_weight: float32 [256, 64], replicated
- grad_up_bias: float32 [256], replicated
- grad_down_weight: float32 [64, 256], replicated
- grad_scale: float32 [64], replicated
Inputs may be any that keep to these rules, and one draw needn't show every extreme that they name: seam_partner[i] = (s - i) mod 4096 for one whole number s, so it is its own inverse.
All inputs are finite; a program needn't handle non-finite values. No bound on the sum of `ocean_mask` on one device may be relied on, other than what follows from the above.
Results may differ from a plain program's by a relative error of at most 0.0068.
Values may be sent and summed in bfloat16 or wider, within the bound.
A program may use at most 64 MiB of HBM per device.

v0:
```python
import math

import jax
import jax.numpy as jnp
from jax import lax
from jax.sharding import PartitionSpec as P


def extended_2(cells, sides, width, closed):
    for axis, dim in sides:
        count = lax.axis_size(axis)
        ends = count if closed else count - 1
        head = lax.slice_in_dim(cells, 0, width, axis=dim)
        tail = lax.slice_in_dim(cells, cells.shape[dim] - width, cells.shape[dim], axis=dim)
        cells = jnp.concatenate(
            [
                lax.ppermute(tail, axis, [(i, (i + 1) % count) for i in range(ends)]),
                cells,
                lax.ppermute(head, axis, [((i + 1) % count, i) for i in range(ends)]),
            ],
            axis=dim,
        )
    return cells


def gelu_slope(pre):
    cdf = 0.5 * (1.0 + lax.erf(pre / math.sqrt(2.0)))
    return cdf + pre * jnp.exp(-0.5 * pre * pre) / math.sqrt(2.0 * math.pi)


def cell_terms(
    conv, field, cot, mask, norm_gain, layer_norm_bias, up_weight, up_bias, down_weight, layer_scale
):
    mean_c = jnp.mean(conv, axis=0, keepdims=True)
    centered_input = conv - mean_c
    var_c = jnp.mean(centered_input * centered_input, axis=0, keepdims=True)
    reciprocal_deviation = lax.rsqrt(var_c + 1e-06)
    standardized_input = centered_input * reciprocal_deviation
    layer_norm_gain = norm_gain.astype(jnp.float32)[:, None]
    normalized_output = (
        standardized_input * layer_norm_gain + layer_norm_bias.astype(jnp.float32)[:, None]
    ).astype(jnp.bfloat16)
    pre = (
        jnp.dot(up_weight, normalized_output, preferred_element_type=jnp.float32)
        + up_bias.astype(jnp.float32)[:, None]
    )
    hidden = jax.nn.gelu(pre, approximate=False).astype(jnp.bfloat16)
    branch = jnp.dot(down_weight, hidden, preferred_element_type=jnp.float32)
    scale = layer_scale.astype(jnp.float32)[:, None]
    out = (mask * (field.astype(jnp.float32) + scale * branch)).astype(jnp.bfloat16)
    grad_in = mask * cot.astype(jnp.float32)
    d_branch = (grad_in * scale).astype(jnp.bfloat16)
    g_scale = jnp.sum(grad_in * branch, axis=1)
    contract_cells = (((1,), (1,)), ((), ()))
    contract_first = (((0,), (0,)), ((), ()))
    g_down = lax.dot_general(d_branch, hidden, contract_cells, preferred_element_type=jnp.float32)
    d_hidden = lax.dot_general(
        down_weight, d_branch, contract_first, preferred_element_type=jnp.float32
    )
    d_pre = (d_hidden * gelu_slope(pre)).astype(jnp.bfloat16)
    g_up_b = jnp.sum(d_pre.astype(jnp.float32), axis=1)
    g_up_w = lax.dot_general(
        d_pre, normalized_output, contract_cells, preferred_element_type=jnp.float32
    )
    normalized_gradient = lax.dot_general(
        up_weight, d_pre, contract_first, preferred_element_type=jnp.float32
    )
    gain_gradient = jnp.sum(normalized_gradient * standardized_input, axis=1)
    g_bias = jnp.sum(normalized_gradient, axis=1)
    gradient_through_norm = normalized_gradient * layer_norm_gain
    convolution_gradient = reciprocal_deviation * (
        gradient_through_norm
        - jnp.mean(gradient_through_norm, axis=0, keepdims=True)
        - standardized_input
        * jnp.mean(gradient_through_norm * standardized_input, axis=0, keepdims=True)
    )
    return (
        out,
        convolution_gradient.astype(jnp.bfloat16),
        (gain_gradient, g_bias, g_up_w, g_up_b, g_down, g_scale),
    )


def make_picker(wanted, carry, piece):
    width = piece.shape[3]
    inside = (wanted >= 0) & (wanted < width)
    picked = jnp.take(piece, jnp.clip(wanted, 0, width - 1), axis=3)
    return jnp.where(inside[None, None, None, :], picked, carry)


def shards(
    fields,
    cotangent,
    ocean_mask,
    seam_partner,
    depth_weight,
    norm_gain,
    layer_norm_bias,
    up_weight,
    up_bias,
    down_weight,
    layer_scale,
):
    samples, chans, rows, cols = fields.shape
    total_lon = seam_partner.shape[0]
    lon_start = lax.axis_index("lon") * cols
    positions = (lon_start + jnp.arange(-3, cols + 3, dtype=jnp.int32)) % total_lon
    partner_cols = jnp.take(seam_partner, positions)
    own_partner = partner_cols[3 : cols + 3]
    is_top = lax.axis_index("lat") == lax.axis_size("lat") - 1
    weight_f = depth_weight.astype(jnp.float32)
    mask_f = ocean_mask.astype(jnp.float32)
    lon_padded = extended_2(fields, (("lon", 3),), 3, True)
    banded = extended_2(lon_padded, (("lat", 2),), 3, False)
    upper = fields[:, :, rows - 3 :, :][:, :, ::-1, :]
    fold_init = jnp.zeros((samples, chans, 3, cols + 6), jnp.bfloat16)
    folded = make_picker(partner_cols, fold_init, lax.all_gather(upper, "lon", axis=3, tiled=True))
    top_rows = jnp.where(is_top, folded, banded[:, :, rows + 3 :, :])
    extended = jnp.concatenate([banded[:, :, : rows + 3, :], top_rows], axis=2)
    conv = jnp.zeros((samples, chans, rows, cols), jnp.float32)
    for row_tap in range(7):
        for col_tap in range(7):
            conv = conv + weight_f[:, row_tap, col_tap][None, :, None, None] * extended[
                :, :, row_tap : row_tap + rows, col_tap : col_tap + cols
            ].astype(jnp.float32)
    mask_flat = mask_f.reshape(1, rows * cols)
    out_s, dconv_s, parts = cell_terms(
        conv[0].reshape(chans, rows * cols),
        fields[0].reshape(chans, rows * cols),
        cotangent[0].reshape(chans, rows * cols),
        mask_flat,
        norm_gain,
        layer_norm_bias,
        up_weight,
        up_bias,
        down_weight,
        layer_scale,
    )
    outputs = [out_s.reshape(chans, rows, cols)]
    dconv_list = [dconv_s.reshape(chans, rows, cols)]
    output = jnp.stack(outputs)
    convolution_gradient = jnp.stack(dconv_list)
    d_conv_f = convolution_gradient.astype(jnp.float32)
    taps = []
    for row_tap in range(7):
        line = []
        for col_tap in range(7):
            line.append(
                jnp.sum(
                    d_conv_f
                    * extended[:, :, row_tap : row_tap + rows, col_tap : col_tap + cols].astype(
                        jnp.float32
                    ),
                    axis=(0, 2, 3),
                )
            )
        taps.append(jnp.stack(line, axis=1))
    g_depth = jnp.stack(taps, axis=1)
    lon_back = extended_2(convolution_gradient, (("lon", 3),), 3, True)
    band_back = extended_2(lon_back, (("lat", 2),), 3, False)
    deeper = jnp.pad(band_back, ((0, 0), (0, 0), (0, 3), (0, 0)))
    spread = jnp.zeros((samples, chans, rows + 3, cols), jnp.float32)
    for row_tap in range(7):
        for col_tap in range(7):
            spread = spread + weight_f[:, row_tap, col_tap][None, :, None, None] * deeper[
                :, :, 6 - row_tap : 9 - row_tap + rows, 6 - col_tap : 6 - col_tap + cols
            ].astype(jnp.float32)
    own = spread[:, :, :rows, :]
    margin = spread[:, :, rows:, :]
    back_init = jnp.zeros((samples, chans, 3, cols), jnp.float32)
    back = make_picker(
        own_partner,
        back_init,
        lax.all_gather(margin.astype(jnp.bfloat16), "lon", axis=3, tiled=True).astype(jnp.float32),
    )
    extra = back[:, :, ::-1, :]
    own = own.at[:, :, rows - 3 :, :].add(jnp.where(is_top, extra, 0.0))
    grad_fields = (mask_f[None, None] * cotangent.astype(jnp.float32) + own).astype(jnp.bfloat16)
    gain_gradient, g_bias, g_up_w, g_up_b, g_down, g_scale = parts
    summed = lax.psum(
        (g_depth, gain_gradient, g_bias, g_up_w, g_up_b, g_down, g_scale), ("lon", "lat")
    )
    return (
        output,
        grad_fields,
        summed[0],
        summed[1],
        summed[2],
        summed[3],
        summed[4],
        summed[5],
        summed[6],
    )


def solution(mesh):
    placed = (
        P(None, None, "lat", "lon"),
        P(None, None, "lat", "lon"),
        P("lat", "lon"),
        P(),
        P(),
        P(),
        P(),
        P(),
        P(),
        P(),
        P(),
    )
    return jax.shard_map(
        shards,
        mesh=mesh,
        in_specs=placed,
        out_specs=(
            P(None, None, "lat", "lon"),
            P(None, None, "lat", "lon"),
            P(),
            P(),
            P(),
            P(),
            P(),
            P(),
            P(),
        ),
        check_vma=False,
    )
```

profile of v0, /device:TPU:1, one launch (start us, length us, event | category | flops | bytes accessed | tf_op | source)
XLA Modules:
  0.0 497.8 jit_solution(14033838073368291433)
XLA Ops:
  9.0 1.5 copy.94
  10.5 7.2 %collective-permute-start = (bf16[1,64,16,3]{1,2,3,0:T(8,128)(2,1)S(1)}, bf16[1,64,16,3]{1,2,3,0:T(8,128)(2,1)S(1)}, u32[]{:S(2)}, u32[]{:S(2)}) collective-permute-start(bf16[1,64,16,3]{1,2,3,0:T(8,128)(2,1)S(1)} %get-tuple-element.147), channel_id=1, source_target_pairs={{0,16},{16,32},{32,48},{48,64},{64,80},{80,96},{96,112},{112,128},... | collective-permute-start | bytes 18440 | tf_op jit(solution)/shard_map/ppermute | solution.py:17
  17.7 3.5 collective-permute-start.1
  22.0 2.0 gather_fusion
  28.9 1.4 copy.95
  33.5 4.2 collective-permute-start.2
  37.7 42.1 %all-gather.3.cloned.1.call-done = bf16[1,64,3,4096]{3,1,2,0:T(8,128)(2,1)} async-done(((bf16[1,64,3,128]{3,1,2,0:T(8,128)(2,1)}), bf16[1,64,3,4096]{3,1,2,0:T(8,128)(2,1)}) %all-gather.3.cloned.1.call-update) | async-done | bytes 1572880 | tf_op jit(solution)/shard_map/all_gather | solution.py:117
  79.8 6.4 %copy.102 = bf16[1,64,3,4096]{1,2,3,0:T(4,128)(2,1)} copy(bf16[1,64,3,4096]{3,1,2,0:T(8,128)(2,1)} %all-gather.3.cloned.1.call-done) | data formatting | bytes 3145728 | tf_op jit(solution)/shard_map/all_gather | solution.py:117
  86.2 3.0 gather_fusion.1
  90.4 10.0 %fusion.134 = (f32[16,128]{0,1:T(8,128)S(1)}, f32[1,64,16,128]{1,2,3,0:T(8,128)S(1)}) fusion(bf16[1,64,19,134]{1,2,3,0:T(8,128)(2,1)S(1)} %get-tuple-element.142, f32[64]{0:T(128)S(1)} %get-tuple-element.152, f32[64]{0:T(128)S(1)} %get-tuple-element.153, f32[64]{0:T(128)S(1)} %get-tuple-element.154, f32[64]{0:T(128)S(1)} %get-tuple-element.155, ...), kind=kLoop, calls=%fused_computation.375 | loop fusion | flops 20051968 | bytes 11829504 | tf_op jit(solution)/shard_map/reduce_sum | solution.py:34
  100.4 1.3 copy.103
  102.8 6.9 %fusion.5 = (bf16[256,2048]{0,1:T(8,128)(2,1)}, f32[256,2048]{0,1:T(8,128)S(1)}) fusion(f32[256]{0:T(256)S(1)} %copy-done.99, bf16[256,64]{0,1:T(8,128)(2,1)S(1)} %copy-done, f32[64]{0:T(128)S(1)} %copy-done.94, f32[64]{0:T(128)S(1)} %copy-done.85, f32[2048]{0:T(1024)S(1)} %rsqrt_bitcast_fusion, f32[2048]{0:T(1024)S(1)} %get-tuple-element.202, ...), kind=kOutput, calls=%fused_computation.63 | convolution fusion | flops 102367232 | bytes 3720704 | tf_op jit(solution)/shard_map/dot_general | solution.py:44
  109.7 2.0 convert_reduce_fusion
  115.9 4.1 fusion.113
  120.2 3.2 collective-permute-start.4
  123.4 2.1 collective-permute-start.5
  125.5 1.6 fusion.112
  127.1 7.3 %collective-permute-done.5 = bf16[1,64,16,3]{3,1,2,0:T(8,128)(2,1)S(1)} collective-permute-done((bf16[1,64,16,3]{3,1,2,0:T(8,128)(2,1)S(1)}, bf16[1,64,16,3]{3,1,2,0:T(8,128)(2,1)S(1)}, u32[]{:S(2)}, u32[]{:S(2)}) %collective-permute-start.5) | collective-permute-done | bytes 6176 | tf_op jit(solution)/shard_map/ppermute | solution.py:19
  135.2 1.9 collective-permute-start.6
  145.2 1.4 pad_maximum_fusion.1
  146.7 1.8 pad_maximum_fusion.2
  148.7 6.7 %multiply_add_fusion = f32[1,64,19,128]{3,1,2,0:T(8,128)S(1)} fusion(bf16[1,64,19,134]{3,1,2,0:T(8,128)(2,1)S(1)} %get-tuple-element.138, bf16[1,64,22,134]{3,1,2,0:T(8,128)(2,1)S(1)} %pad_maximum_fusion.1, bf16[1,64,19,134]{3,1,2,0:T(8,128)(2,1)S(1)} %get-tuple-element.137, f32[64]{0:T(128)S(1)} %copy-done.53, f32[64]{0:T(128)S(1)} %copy-done.55, ...), kind=kLoop, calls=%fused_computation.239 | loop fusion | flops 22724608 | bytes 10078720 | tf_op jit(solution)/shard_map/add | solution.py:165
  158.3 3.9 fusion.85
  164.5 1.7 fusion.132
  166.1 2.3 fusion.133
  168.5 107.1 %all-reduce.1 = (f32[64,7,7]{0,2,1:T(8,128)}, f32[64]{0:T(128)}, f32[64]{0:T(128)}, f32[256]{0:T(256)}, f32[64]{0:T(128)}) all-reduce(f32[64,7,7]{0,2,1:T(8,128)S(1)} %constant_dynamic-update-slice_fusion, f32[64]{0:T(128)S(1)} %copy-done.92, f32[64]{0:T(128)S(1)} %copy-done.91, ...), channel_id=1, replica_groups=mesh['lon'=32,'lat'=16] {'lon','lat'}, use_global_device_ids=true, to_apply=%region_53.54 | all-reduce | flops 3584 | bytes 28672 | tf_op jit(solution)/shard_map/psum | solution.py:180
  275.6 6.4 %copy.112 = bf16[1,64,3,4096]{1,2,3,0:T(4,128)(2,1)} copy(bf16[1,64,3,4096]{3,1,2,0:T(8,128)(2,1)} %all-gather.5.cloned.1.call-done) | data formatting | bytes 3145728 | tf_op jit(solution)/shard_map/all_gather | solution.py:174
  282.1 6.3 %bitcast_convert_fusion = f32[64,3,4096]{0,1,2:T(4,128)} fusion(bf16[1,64,3,4096]{1,2,3,0:T(4,128)(2,1)} %copy.112), kind=kLoop, calls=%fused_computation.52 | loop fusion | flops 786432 | bytes 4718592 | tf_op jit(solution)/shard_map/convert_element_type | solution.py:174
  288.3 4.3 gather_fusion.2
  293.8 194.5 %all-reduce.5.cloned.1.call-done = (f32[256,64]{0,1:T(8,128)}, f32[64,256]{1,0:T(8,128)}) async-done(((f32[256,64]{0,1:T(8,128)}, f32[64,256]{1,0:T(8,128)}), (f32[256,64]{0,1:T(8,128)}, f32[64,256]{1,0:T(8,128)})) %all-reduce.5.cloned.1.call-update) | async-done | bytes 131088 | tf_op jit(solution)/shard_map/psum | solution.py:180
  488.3 1.5 copy.159
  489.8 1.5 copy.160
  (282 shorter events, 31.4 us)
Async XLA Ops:
  7.2 95.5 %copy-start = (bf16[256,64]{0,1:T(8,128)(2,1)S(1)}, bf16[256,64]{0,1:T(8,128)(2,1)}, u32[]{:S(2)}) copy-start(bf16[256,64]{0,1:T(8,128)(2,1)} %param.20) | copy-start | bytes 98308
  7.2 72.6 %all-gather.3.cloned.1.call-start = ((), (), s32[]{:S(2)}) async-start(), calls=%async_computation | async-start | bytes 1622016 | tf_op jit(solution)/shard_map/all_gather | solution.py:117
  8.9 266.7 %all-gather.5.cloned.1.call-start = ((), (), s32[]{:S(2)}) async-start(), calls=%async_computation.1 | async-start | bytes 1622016 | tf_op jit(solution)/shard_map/all_gather | solution.py:174
  10.5 16.3 %collective-permute-start = (bf16[1,64,16,3]{1,2,3,0:T(8,128)(2,1)S(1)}, bf16[1,64,16,3]{1,2,3,0:T(8,128)(2,1)S(1)}, u32[]{:S(2)}, u32[]{:S(2)}) collective-permute-start(bf16[1,64,16,3]{1,2,3,0:T(8,128)(2,1)S(1)} %get-tuple-element.147), channel_id=1, source_target_pairs={{0,16},{16,32},{32,48},{48,64},{64,80},{80,96},{96,112},{112,128},... | collective-permute-start | bytes 18440 | tf_op jit(solution)/shard_map/ppermute | solution.py:17
  17.7 9.1 %collective-permute-start.1 = (bf16[1,64,16,3]{1,2,3,0:T(8,128)(2,1)S(1)}, bf16[1,64,16,3]{1,2,3,0:T(8,128)(2,1)S(1)}, u32[]{:S(2)}, u32[]{:S(2)}) collective-permute-start(bf16[1,64,16,3]{1,2,3,0:T(8,128)(2,1)S(1)} %get-tuple-element.148), channel_id=1, source_target_pairs={{16,0},{32,16},{48,32},{64,48},{80,64},{96,80},{112,96},{128,112},... | collective-permute-start | bytes 18440 | tf_op jit(solution)/shard_map/ppermute | solution.py:19
  24.7 65.4 %copy-start.28 = (f32[64]{0:T(128)}, f32[64]{0:T(128)S(1)}, u32[]{:S(2)}) copy-start(f32[64]{0:T(128)S(1)} %get-tuple-element.189) | copy-start | bytes 772
  24.7 65.4 %copy-start.30 = (f32[64]{0:T(128)}, f32[64]{0:T(128)S(1)}, u32[]{:S(2)}) copy-start(f32[64]{0:T(128)S(1)} %get-tuple-element.190) | copy-start | bytes 772
  24.7 65.4 %copy-start.32 = (f32[64]{0:T(128)}, f32[64]{0:T(128)S(1)}, u32[]{:S(2)}) copy-start(f32[64]{0:T(128)S(1)} %get-tuple-element.191) | copy-start | bytes 772
  24.7 65.4 %copy-start.34 = (f32[64]{0:T(128)}, f32[64]{0:T(128)S(1)}, u32[]{:S(2)}) copy-start(f32[64]{0:T(128)S(1)} %get-tuple-element.192) | copy-start | bytes 772
  24.7 65.4 %copy-start.36 = (f32[64]{0:T(128)}, f32[64]{0:T(128)S(1)}, u32[]{:S(2)}) copy-start(f32[64]{0:T(128)S(1)} %get-tuple-element.193) | copy-start | bytes 772
  24.7 65.4 %copy-start.38 = (f32[64]{0:T(128)}, f32[64]{0:T(128)S(1)}, u32[]{:S(2)}) copy-start(f32[64]{0:T(128)S(1)} %get-tuple-element.194) | copy-start | bytes 772
  24.7 65.4 %copy-start.40 = (f32[64]{0:T(128)}, f32[64]{0:T(128)S(1)}, u32[]{:S(2)}) copy-start(f32[64]{0:T(128)S(1)} %get-tuple-element.195) | copy-start | bytes 772
  24.8 65.4 %copy-start.42 = (f32[64]{0:T(128)}, f32[64]{0:T(128)S(1)}, u32[]{:S(2)}) copy-start(f32[64]{0:T(128)S(1)} %get-tuple-element.196) | copy-start | bytes 772
  24.8 65.4 %copy-start.44 = (f32[64]{0:T(128)}, f32[64]{0:T(128)S(1)}, u32[]{:S(2)}) copy-start(f32[64]{0:T(128)S(1)} %get-tuple-element.197) | copy-start | bytes 772
  24.8 65.4 %copy-start.46 = (f32[64]{0:T(128)}, f32[64]{0:T(128)S(1)}, u32[]{:S(2)}) copy-start(f32[64]{0:T(128)S(1)} %get-tuple-element.198) | copy-start | bytes 772
  24.8 65.4 %copy-start.48 = (f32[64]{0:T(128)}, f32[64]{0:T(128)S(1)}, u32[]{:S(2)}) copy-start(f32[64]{0:T(128)S(1)} %get-tuple-element.199) | copy-start | bytes 772
  25.4 64.8 %copy-start.54 = (f32[64]{0:T(128)}, f32[64]{0:T(128)S(1)}, u32[]{:S(2)}) copy-start(f32[64]{0:T(128)S(1)} %get-tuple-element.153) | copy-start | bytes 772
  25.4 64.8 %copy-start.56 = (f32[64]{0:T(128)}, f32[64]{0:T(128)S(1)}, u32[]{:S(2)}) copy-start(f32[64]{0:T(128)S(1)} %get-tuple-element.154) | copy-start | bytes 772
  25.4 64.8 %copy-start.58 = (f32[64]{0:T(128)}, f32[64]{0:T(128)S(1)}, u32[]{:S(2)}) copy-start(f32[64]{0:T(128)S(1)} %get-tuple-element.155) | copy-start | bytes 772
  25.4 64.8 %copy-start.60 = (f32[64]{0:T(128)}, f32[64]{0:T(128)S(1)}, u32[]{:S(2)}) copy-start(f32[64]{0:T(128)S(1)} %get-tuple-element.156) | copy-start | bytes 772
  25.4 64.8 %copy-start.62 = (f32[64]{0:T(128)}, f32[64]{0:T(128)S(1)}, u32[]{:S(2)}) copy-start(f32[64]{0:T(128)S(1)} %get-tuple-element.157) | copy-start | bytes 772
  25.5 64.8 %copy-start.64 = (f32[64]{0:T(128)}, f32[64]{0:T(128)S(1)}, u32[]{:S(2)}) copy-start(f32[64]{0:T(128)S(1)} %get-tuple-element.158) | copy-start | bytes 772
  25.5 64.8 %copy-start.66 = (f32[64]{0:T(128)}, f32[64]{0:T(128)S(1)}, u32[]{:S(2)}) copy-start(f32[64]{0:T(128)S(1)} %get-tuple-element.159) | copy-start | bytes 772
  25.5 64.8 %copy-start.68 = (f32[64]{0:T(128)}, f32[64]{0:T(128)S(1)}, u32[]{:S(2)}) copy-start(f32[64]{0:T(128)S(1)} %get-tuple-element.160) | copy-start | bytes 772
  26.8 82.9 %copy-start.18 = (f32[2048]{0:T(1024)}, f32[2048]{0:T(1024)S(1)}, u32[]{:S(2)}) copy-start(f32[2048]{0:T(1024)S(1)} %get-tuple-element.201) | copy-start | bytes 24580
  27.0 62.2 %collective-permute-start.3 = (bf16[1,64,3,134]{1,2,3,0:T(4,128)(2,1)S(1)}, bf16[1,64,3,134]{1,2,3,0:T(4,128)(2,1)S(1)}, u32[]{:S(2)}, u32[]{:S(2)}) collective-permute-start(bf16[1,64,3,134]{1,2,3,0:T(4,128)(2,1)S(1)} %get-tuple-element.144), channel_id=1, source_target_pairs={{1,0},{2,1},{3,2},{4,3},{5,4},{6,5},{7,6},{8,7},{9,8},{10,9},{11,1... | collective-permute-start | bytes 154376 | tf_op jit(solution)/shard_map/ppermute | solution.py:19
  33.5 56.1 %collective-permute-start.2 = (bf16[1,64,3,134]{1,2,3,0:T(4,128)(2,1)S(1)}, bf16[1,64,3,134]{1,2,3,0:T(4,128)(2,1)S(1)}, u32[]{:S(2)}, u32[]{:S(2)}) collective-permute-start(bf16[1,64,3,134]{1,2,3,0:T(4,128)(2,1)S(1)} %get-tuple-element.143), channel_id=1, source_target_pairs={{0,1},{1,2},{2,3},{3,4},{4,5},{5,6},{6,7},{7,8},{8,9},{9,10},{10,1... | collective-permute-start | bytes 154376 | tf_op jit(solution)/shard_map/ppermute | solution.py:17
  120.2 6.9 %collective-permute-start.4 = (bf16[1,64,16,3]{3,1,2,0:T(8,128)(2,1)S(1)}, bf16[1,64,16,3]{3,1,2,0:T(8,128)(2,1)S(1)}, u32[]{:S(2)}, u32[]{:S(2)}) collective-permute-start(bf16[1,64,16,3]{3,1,2,0:T(8,128)(2,1)S(1)} %get-tuple-element.149), channel_id=1, source_target_pairs={{0,16},{16,32},{32,48},{48,64},{64,80},{80,96},{96,112},{112,128},... | collective-permute-start | bytes 18440 | tf_op jit(solution)/shard_map/ppermute | solution.py:17
  123.4 11.0 %collective-permute-start.5 = (bf16[1,64,16,3]{3,1,2,0:T(8,128)(2,1)S(1)}, bf16[1,64,16,3]{3,1,2,0:T(8,128)(2,1)S(1)}, u32[]{:S(2)}, u32[]{:S(2)}) collective-permute-start(bf16[1,64,16,3]{3,1,2,0:T(8,128)(2,1)S(1)} %get-tuple-element.150), channel_id=1, source_target_pairs={{16,0},{32,16},{48,32},{64,48},{80,64},{96,80},{112,96},{128,112},... | collective-permute-start | bytes 18440 | tf_op jit(solution)/shard_map/ppermute | solution.py:19
  135.2 10.0 %collective-permute-start.6 = (bf16[1,64,3,134]{3,1,2,0:T(8,128)(2,1)}, bf16[1,64,3,134]{3,1,2,0:T(8,128)(2,1)}, u32[]{:S(2)}, u32[]{:S(2)}) collective-permute-start(bf16[1,64,3,134]{3,1,2,0:T(8,128)(2,1)} %get-tuple-element.140), channel_id=1, source_target_pairs={{0,1},{1,2},{2,3},{3,4},{4,5},{5,6},{6,7},{7,8},{8,9},{9,10},{10,1... | collective-permute-start | bytes 154376 | tf_op jit(solution)/shard_map/ppermute | solution.py:17
  137.2 8.1 %collective-permute-start.7 = (bf16[1,64,3,134]{3,1,2,0:T(8,128)(2,1)}, bf16[1,64,3,134]{3,1,2,0:T(8,128)(2,1)}, u32[]{:S(2)}, u32[]{:S(2)}) collective-permute-start(bf16[1,64,3,134]{3,1,2,0:T(8,128)(2,1)} %get-tuple-element.139), channel_id=1, source_target_pairs={{1,0},{2,1},{3,2},{4,3},{5,4},{6,5},{7,6},{8,7},{9,8},{10,9},{11,1... | collective-permute-start | bytes 154376 | tf_op jit(solution)/shard_map/ppermute | solution.py:19
  156.9 331.4 %all-reduce.5.cloned.1.call-start = ((), (), s32[]{:S(2)}) async-start(), calls=%async_computation.2 | async-start | bytes 262144 | tf_op jit(solution)/shard_map/psum | solution.py:180
  (80 other events, 922.8 us)
Sparse Core Ops, SparseCore 0:
  11.7 68.0 all-gather.2
  157.0 65.3 all-gather.4
  228.2 260.0 all-reduce.4
where the time goes:
time: 499 us; the launch traced here: 498 us
  waiting for transfers between devices  244 us (49%)
  blocking collectives  107 us (21%)
  local copies, waits for them, and re-layouts  46.1 us (9%)
  other arithmetic  45.4 us (9%)
  starting transfers between devices  24.7 us (5%)
  between operations  15.4 us (3%)
  matrix products  15.1 us (3%)
    psum x1, waiting for transfers between devices, shards(): lax.psum((g_depth, gain_gradient, g_bias, g_up_w, g_up_b, g_down, g_scale...  195 us
    psum x1, blocking collectives, shards(): lax.psum((g_depth, gain_gradient, g_bias, g_up_w, g_up_b, g_down, g_scale...  107 us
    all_gather x1, waiting for transfers between devices, shards(): lax.all_gather(upper, 'lon', axis=3, tiled=True)  42.1 us
    ppermute x4, starting transfers between devices, extended_2(): lax.ppermute(tail, axis, [(i, (i + 1) % count) for i in range(ends)])  16.4 us
    reduce_sum x4, other arithmetic, shards(): jnp.sum(d_conv_f * extended[:, :, row_tap:row_tap + rows, col_tap:col_tap...  10.9 us
    reduce_sum x1, other arithmetic, cell_terms(): mean_c = jnp.mean(conv, axis=0, keepdims=True)  9.98 us
  transfers between devices with their start and end apart: 11, of which 3 were waited for; matrix products, arithmetic and copies ran while one was open for 12% of the time, Pallas kernels for 0%

commit v1 on v0

v1 whole, which is shorter than its diff:
```python
import functools
import math

import jax
import jax.numpy as jnp
from jax import lax
from jax.experimental import pallas as pl
from jax.experimental.pallas import tpu as pltpu
from jax.sharding import PartitionSpec as P

F32 = jnp.float32
BF16 = jnp.bfloat16
MESH = pl.DeviceIdType.MESH
C = 64
R = 16
L = 128
HID = 256
RE = R + 6
AR_ROWS = 384
AR_DOWN = 144
AR_DEPTH = 288
CORES = 2

ERF_P = 0.3275911 / math.sqrt(2.0)
ERF_C = (
    0.5 * 0.254829592,
    0.5 * -0.284496736,
    0.5 * 1.421413741,
    0.5 * -1.453152027,
    0.5 * 1.061405429,
)
PDF = 1.0 / math.sqrt(2.0 * math.pi)


def phi_and_density(v):
    d = 1.0 + ERF_P * jnp.abs(v)
    t = pl.reciprocal(d, approx=True)
    t = t * (2.0 - d * t)
    e = jnp.exp(-0.5 * (v * v))
    poly = ERF_C[4]
    for coef in ERF_C[3::-1]:
        poly = poly * t + coef
    tail = poly * t * e
    return jnp.where(v >= 0.0, 1.0 - tail, tail), e


def nt_dot(a, b):
    return lax.dot_general(a, b, (((1,), (1,)), ((), ())), preferred_element_type=F32)


def dot(a, b):
    return jnp.dot(a, b, preferred_element_type=F32)


def roll(x, amount):
    amount %= L
    return pltpu.roll(x, amount, x.ndim - 1) if amount else x


def kernel(
    dims,
    fields_ref,
    cot_ref,
    mask_ref,
    seam_ref,
    par_ref,
    upx_ref,
    up_ref,
    down_ref,
    out_ref,
    gf_ref,
    ar_ref,
    rows_f,
    gmask,
    outr,
    xm,
    dm,
    shifts,
    hal,
    fshift,
    wts,
    conv,
    pks,
    pkr,
    fx,
    fzs,
    fzr,
    onehot,
    upt,
    downt,
    parb,
    acc_s,
    acc_down,
    acc_up,
    ar_src,
    ar1,
    ar2,
    ar3,
    ag,
    halo_send,
    halo_recv,
    fx_send,
    fx_recv,
    fz_send,
    fz_recv,
    a1_send,
    a1_recv,
    a2_send,
    a2_recv,
    a3_send,
    a3_recv,
    ag_send,
    ag_recv,
):
    nlon, nlat, nx = dims
    nzc = nlon // nx
    nz = nzc // CORES
    ng = nx * CORES
    chunk = AR_ROWS // nlat
    early = AR_DEPTH // chunk
    lon = lax.axis_index("lon")
    lat = lax.axis_index("lat")
    mx, mzc = lon // nzc, lon % nzc
    mz, mc = mzc // CORES, mzc % CORES
    mg = mx * CORES + mc
    left, right = (lon + nlon - 1) % nlon, (lon + 1) % nlon
    down_lat, up_lat = (lat + nlat - 1) % nlat, (lat + 1) % nlat
    lats = (down_lat, lat, up_lat)
    is_top = lat == nlat - 1
    is_bottom = lat == 0

    def place(a, b):
        return {"lon": a, "lat": b}

    def lon_of_group(g):
        return (g // CORES) * nzc + mz * CORES + g % CORES

    barrier = pltpu.get_barrier_semaphore()

    def hail(a, b):
        pl.semaphore_signal(barrier, inc=1, device_id=place(a, b), device_id_type=MESH)

    for b in lats:
        hail(left, b)
        hail(right, b)
    hail(lon, down_lat)
    hail(lon, up_lat)

    @pl.loop(1, nlat)
    def _(j):
        hail(lon, (lat + j) % nlat)

    @pl.loop(1, ng)
    def _(j):
        hail(lon_of_group((mg + j) % ng), lat)

    @pl.loop(1, nzc)
    def _(j):
        hail(mx * nzc + (mzc + j) % nzc, lat)

    lane = lax.broadcasted_iota(jnp.int32, (C, L), 1)
    slot_of_lane = lane // 8
    low_half = lane < 64

    def remote(src, dst, send, recv, where):
        return pltpu.make_async_remote_copy(
            src_ref=src, dst_ref=dst, send_sem=send, recv_sem=recv,
            device_id=where, device_id_type=MESH,
        )

    def halo_copies(ph, rows):
        made = [
            remote(rows.at[pl.ds(3, 3)], rows.at[pl.ds(R + 3, 3)],
                   halo_send.at[ph, 0], halo_recv.at[ph, 0], place(lon, down_lat)),
            remote(rows.at[pl.ds(R, 3)], rows.at[pl.ds(0, 3)],
                   halo_send.at[ph, 1], halo_recv.at[ph, 1], place(lon, up_lat)),
        ]
        for side, to in ((0, left), (1, right)):
            for k in range(3):
                sem = 2 + 3 * side + k
                made.append(
                    remote(pks.at[ph, side], pkr.at[ph, side, k],
                           halo_send.at[ph, sem], halo_recv.at[ph, sem], place(to, lats[k]))
                )
        return made

    def pack(ph, row):
        low = jnp.zeros((C, L), F32)
        high = jnp.zeros((C, L), F32)
        for i in range(R):
            here = slot_of_lane == i
            low = jnp.where(here, roll(row(i), 8 * i), low)
            high = jnp.where(here, roll(row(i), 8 * i + 8), high)
        pks[ph, 0] = low.astype(BF16)
        pks[ph, 1] = high.astype(BF16)

    def unpack(ph):
        for k, ext_rows, first in ((2, range(0, 3), 13), (1, range(3, R + 3), -3), (0, range(R + 3, RE), -R - 3)):
            from_right = pkr[ph, 0, k].astype(F32)
            from_left = pkr[ph, 1, k].astype(F32)
            for u in ext_rows:
                i = u + first
                hal[u] = jnp.where(low_half, roll(from_right, -8 * i), roll(from_left, 120 - 8 * i))

    def shifted(q, main, halo, lanes):
        if q == 3:
            return main
        edge = lanes >= 125 + q if q < 3 else lanes < q - 3
        return roll(jnp.where(edge, halo, main), 3 - q)

    def build_shifts(rows):
        @pl.loop(0, C // 16)
        def _(s):
            cs = pl.ds(pl.multiple_of(s * 16, 16), 16)
            main = rows[:, cs, :].astype(F32)
            halo = hal[:, cs, :]
            lanes = lax.broadcasted_iota(jnp.int32, (RE, 16, L), 2)
            for q in range(7):
                shifts[q, :, cs, :] = shifted(q, main, halo, lanes)

    def fold_first(ph, rows):
        fx[ph, mx] = rows[R : R + 3]

        @pl.loop(1, nx)
        def _(j):
            to = (mx + j) % nx
            remote(rows.at[pl.ds(R, 3)], fx.at[ph, mx], fx_send.at[ph, to], fx_recv.at[ph, mx],
                   place(to * nzc + mzc, lat)).start()

    def fold_second(ph, rows):
        @pl.loop(1, nx)
        def _(j):
            to = (mx + j) % nx
            remote(rows.at[pl.ds(R, 3)], fx.at[ph, to], fx_send.at[ph, to], fx_recv.at[ph, to],
                   place(to * nzc + mzc, lat)).wait()

        held = jnp.concatenate([fx[ph, x].reshape(3 * C, L) for x in range(nx)], axis=1)

        @pl.loop(0, nzc)
        def _(t):
            got = dot(held, onehot[t])
            mirrored = [got[C * (2 - k) : C * (3 - k)] for k in range(3)]
            slot = slot_of_lane % 8
            edges = mirrored[2][:, L:]
            for k in (1, 0):
                edges = jnp.where(slot == k, mirrored[k][:, L:], edges)
            for k in range(3):
                fzs[ph, t, k] = mirrored[k][:, :L].astype(BF16)
            fzs[ph, t, 3] = edges.astype(BF16)

        fzr[ph, mzc] = fzs[ph, mzc]

        @pl.loop(1, nzc)
        def _(j):
            t = (mzc + j) % nzc
            remote(fzs.at[ph, t], fzr.at[ph, mzc], fz_send.at[ph, t], fz_recv.at[ph, mzc],
                   place(mx * nzc + t, lat)).start()

    def fold_last(ph):
        @pl.loop(1, nzc)
        def _(j):
            t = (mzc + j) % nzc
            remote(fzs.at[ph, t], fzr.at[ph, t], fz_send.at[ph, t], fz_recv.at[ph, t],
                   place(mx * nzc + t, lat)).wait()

        total = fzr[ph, 0].astype(F32)
        for t in range(1, nzc):
            total = total + fzr[ph, t].astype(F32)
        halos = [
            jnp.where(low_half, roll(total[3], -8 * k), roll(total[3], 56 - 8 * k))
            for k in range(3)
        ]
        return [total[k] for k in range(3)], halos

    rows_f[...] = fields_ref[...].astype(F32).reshape(C * R, L)
    for i in range(R):
        xm[3 + i] = rows_f[pl.ds(i, C, stride=R), :].astype(BF16)
    pack(0, lambda i: xm[3 + i].astype(F32))
    pl.semaphore_wait(barrier, 8 + (nlat - 1) + (ng - 1) + (nzc - 1))
    sent = halo_copies(0, xm)
    for copy in sent:
        copy.start()

    @pl.when(is_top)
    def _():
        fold_first(0, xm)
        partner = seam_ref[0:1, 0:1]
        rows_i = lax.broadcasted_iota(jnp.int32, (nx * L, 2 * L), 0)
        held_col = L * ((rows_i // L) * nzc + mzc) + rows_i % L
        col = lax.broadcasted_iota(jnp.int32, (1, 2 * L), 1)
        packed = col - L
        ahead = jnp.where(packed < 64, L + packed % 8, packed % 8 - 8)
        offset = jnp.where(col < L, col, ahead)

        @pl.loop(0, nzc)
        def _(t):
            wanted = (partner - L * (mx * nzc + t) - offset) & (nlon * L - 1)
            onehot[t] = jnp.where(held_col == wanted, 1.0, 0.0).astype(BF16)

    rows_f[...] = cot_ref[...].astype(F32).reshape(C * R, L)
    for i in range(R):
        gmask[i] = rows_f[pl.ds(i, C, stride=R), :] * mask_ref[i : i + 1, :].astype(F32)
    par = par_ref[...]
    for tap in range(49):
        wts[tap] = jnp.broadcast_to(par[:, tap : tap + 1], (C, L))
    for n in range(3):
        parb[n] = jnp.broadcast_to(par[:, 64 + n : 65 + n], (C, 2 * L))

    def eye(n):
        return jnp.where(
            lax.broadcasted_iota(jnp.int32, (n, n), 0) == lax.broadcasted_iota(jnp.int32, (n, n), 1), 1.0, 0.0
        ).astype(BF16)

    upt[...] = nt_dot(eye(C), up_ref[...]).astype(BF16)
    downt[...] = nt_dot(eye(HID), down_ref[...]).astype(BF16)
    acc_s[...] = jnp.zeros_like(acc_s)
    acc_down[...] = jnp.zeros_like(acc_down)
    acc_up[...] = jnp.zeros_like(acc_up)

    @pl.when(is_top)
    def _():
        fold_second(0, xm)

    for copy in sent:
        copy.wait()
    unpack(0)

    @pl.when(is_bottom)
    def _():
        for u in range(3):
            xm[u] = jnp.zeros((C, L), BF16)
            hal[u] = jnp.zeros((C, L), F32)

    @pl.when(is_top)
    def _():
        mains, halos = fold_last(0)
        for k in range(3):
            xm[R + 3 + k] = mains[k].astype(BF16)
            hal[R + 3 + k] = halos[k]

    build_shifts(xm)

    @pl.loop(0, C // 8)
    def _(s):
        cs = pl.ds(pl.multiple_of(s * 8, 8), 8)
        total = jnp.zeros((R, 8, L), F32)
        for q in range(7):
            for a in range(7):
                total = total + wts[a * 7 + q, cs, :][None] * shifts[q, a : a + R, cs, :]
        conv[:, cs, :] = total

    @pl.loop(0, R // 2)
    def _(r):
        two = pl.ds(2 * r, 2)

        def flat(x):
            return jnp.concatenate([x[0], x[1]], axis=1)

        gain, bias, scale = parb[0], parb[1], parb[2]
        x = flat(conv[two])
        mean = jnp.mean(x, axis=0, keepdims=True)
        x = x - mean
        rstd = lax.rsqrt(jnp.mean(x * x, axis=0, keepdims=True) + 1e-06)
        xhat = x * rstd
        normed = (xhat * gain + bias).astype(BF16)
        normed_one = jnp.concatenate([normed, jnp.ones((16, 2 * L), BF16)], axis=0)
        pre = dot(upx_ref[...], normed_one)
        phi, density = phi_and_density(pre)
        hidden = (pre * phi).astype(BF16)
        slope = phi + pre * density * PDF
        branch = dot(down_ref[...], hidden)
        mask = mask_ref[two, :].astype(F32)
        mask = jnp.concatenate([mask[0:1], mask[1:2]], axis=1)
        field = flat(xm[pl.ds(3 + 2 * r, 2)].astype(F32))
        out = mask * (field + scale * branch)
        outr[2 * r] = out[:, :L]
        outr[2 * r + 1] = out[:, L:]
        g = flat(gmask[two])
        d_branch = (g * scale).astype(BF16)
        acc_s[2] += g * branch
        acc_down[...] += nt_dot(d_branch, hidden)
        d_hidden = dot(downt[...], d_branch)
        d_pre = (d_hidden * slope).astype(BF16)
        acc_up[...] += nt_dot(normed_one, d_pre)
        d_normed = dot(upt[...], d_pre)
        acc_s[0] += d_normed * xhat
        acc_s[1] += d_normed
        gd = d_normed * gain
        d_conv = rstd * (
            gd
            - jnp.mean(gd, axis=0, keepdims=True)
            - xhat * jnp.mean(gd * xhat, axis=0, keepdims=True)
        )
        d_conv = d_conv.astype(BF16)
        dm[3 + 2 * r] = d_conv[:, :L]
        dm[4 + 2 * r] = d_conv[:, L:]
        d_conv = d_conv.astype(F32)
        conv[2 * r] = d_conv[:, :L]
        conv[2 * r + 1] = d_conv[:, L:]

    pack(1, lambda i: conv[i])
    sent = halo_copies(1, dm)
    for copy in sent:
        copy.start()

    @pl.when(is_top)
    def _():
        fold_first(1, dm)

    def chunk_copy(to, slot):
        return remote(
            ar_src.at[pl.ds(pl.multiple_of(to * chunk, 8), chunk)], ar1.at[slot],
            a1_send.at[to], a1_recv.at[slot], place(lon, to),
        )

    def send_chunks(first, last):
        @pl.loop(first, last)
        def _(p):
            @pl.when(p != lat)
            def _():
                chunk_copy(p, lat).start()

    up = acc_up[...]
    ar_src[0:72] = up[:72, :L]
    ar_src[72:144] = up[:72, L:]
    down = acc_down[...]
    ar_src[AR_DOWN : AR_DOWN + C] = down[:, :L]
    ar_src[AR_DOWN + C : AR_DOWN + 2 * C] = down[:, L:]
    ar_src[AR_DOWN + 2 * C : AR_DEPTH] = jnp.zeros((AR_DEPTH - AR_DOWN - 2 * C, L), F32)
    ar_src[AR_DEPTH + C :] = jnp.zeros((AR_ROWS - AR_DEPTH - C, L), F32)
    send_chunks(0, early)

    @pl.when(is_top)
    def _():
        fold_second(1, dm)

    @pl.loop(0, C // 8)
    def _(s):
        cs = pl.ds(pl.multiple_of(s * 8, 8), 8)
        d_conv = conv[:, cs, :]
        lanes = lax.broadcasted_iota(jnp.int32, (8, L), 1)
        got = jnp.zeros((8, L), F32)
        for q in range(7):
            for a in range(7):
                tap = jnp.sum(d_conv * shifts[q, a : a + R, cs, :], axis=0)
                got = jnp.where(lanes == a * 7 + q, jnp.sum(tap, axis=1, keepdims=True), got)
        for n in range(3):
            got = jnp.where(lanes == 64 + n, jnp.sum(acc_s[n, cs, :], axis=1, keepdims=True), got)
        ar_src[pl.ds(pl.multiple_of(AR_DEPTH + s * 8, 8), 8)] = got

    send_chunks(early, nlat)

    for copy in sent:
        copy.wait()
    unpack(1)

    @pl.when(is_bottom)
    def _():
        for u in range(3):
            dm[u] = jnp.zeros((C, L), BF16)
            hal[u] = jnp.zeros((C, L), F32)

    @pl.when(is_top)
    def _():
        for u in range(R + 3, RE):
            dm[u] = jnp.zeros((C, L), BF16)
            hal[u] = jnp.zeros((C, L), F32)

    build_shifts(dm)

    @pl.loop(0, nlat)
    def _(p):
        @pl.when(p != lat)
        def _():
            chunk_copy(p, p).wait()

    own = pl.ds(pl.multiple_of(lat * chunk, 8), chunk)
    ar1[lat] = ar_src[own]
    ar2[mg] = jnp.sum(ar1[...], axis=0)

    def group_copy(j, slot):
        to = (mg + j) % ng
        return remote(ar2.at[mg], ar2.at[slot(to)], a2_send.at[to], a2_recv.at[slot(to)],
                      place(lon_of_group(to), lat))

    @pl.loop(1, ng)
    def _(j):
        group_copy(j, lambda to: mg).start()

    def adjoint(first, last):
        @pl.loop(first, last)
        def _(s):
            cs = pl.ds(pl.multiple_of(s * 8, 8), 8)
            total = gmask[:, cs, :]
            for q in range(7):
                for a in range(7):
                    total = total + wts[a * 7 + q, cs, :][None] * shifts[6 - q, 6 - a : 6 - a + R, cs, :]
            gmask[:, cs, :] = total

    adjoint(0, C // 16)

    @pl.loop(1, ng)
    def _(j):
        group_copy(j, lambda to: to).wait()

    ar3[mz] = jnp.sum(ar2[...], axis=0)

    def depth_copy(j, slot):
        to = (mz + j) % nz
        return remote(ar3.at[mz], ar3.at[slot(to)], a3_send.at[to], a3_recv.at[slot(to)],
                      place(mx * nzc + to * CORES + mc, lat))

    if nz > 1:

        @pl.loop(1, nz)
        def _(j):
            depth_copy(j, lambda to: mz).start()

    adjoint(C // 16, C // 8)

    if nz > 1:

        @pl.loop(1, nz)
        def _(j):
            depth_copy(j, lambda to: to).wait()

    ag[lat] = jnp.sum(ar3[...], axis=0)

    def spread_copy(j, slot):
        to = (lat + j) % nlat
        return remote(ag.at[lat], ag.at[slot(to)], ag_send.at[to], ag_recv.at[slot(to)],
                      place(lon, to))

    @pl.loop(1, nlat)
    def _(j):
        spread_copy(j, lambda to: lat).start()

    for i in range(R):
        rows_f[pl.ds(i, C, stride=R), :] = outr[i]
    out_ref[...] = rows_f[...].reshape(C, R, L).astype(BF16)

    @pl.when(is_top)
    def _():
        mains, halos = fold_last(1)
        for k in range(3):
            for q in range(7):
                fshift[q, k] = shifted(q, mains[k], halos[k], lane)
        for k in range(3):
            total = gmask[R - 1 - k]
            for a in range(k + 4, 7):
                for q in range(7):
                    total = total + wts[a * 7 + q] * fshift[q, a - k - 4]
            gmask[R - 1 - k] = total

    for i in range(R):
        rows_f[pl.ds(i, C, stride=R), :] = gmask[i]
    gf_ref[...] = rows_f[...].reshape(C, R, L).astype(BF16)

    @pl.loop(1, nlat)
    def _(j):
        spread_copy(j, lambda to: to).wait()

    for p in range(nlat):
        ar_ref[p * chunk : (p + 1) * chunk] = ag[p]


def shards(
    dims,
    fields,
    cotangent,
    ocean_mask,
    seam_partner,
    depth_weight,
    norm_gain,
    layer_norm_bias,
    up_weight,
    up_bias,
    down_weight,
    layer_scale,
):
    nlon, nlat, nx = dims
    nzc = nlon // nx
    nz = nzc // CORES
    ng = nx * CORES
    chunk = AR_ROWS // nlat
    params = jnp.concatenate(
        [
            depth_weight.reshape(C, 49),
            jnp.zeros((C, 15), BF16),
            norm_gain[:, None],
            layer_norm_bias[:, None],
            layer_scale[:, None],
            jnp.zeros((C, 61), BF16),
        ],
        axis=1,
    ).astype(F32)
    up_ext = jnp.concatenate([up_weight, up_bias[:, None], jnp.zeros((HID, 15), BF16)], axis=1)
    vmem = pl.BlockSpec(memory_space=pltpu.VMEM)
    dma = pltpu.SemaphoreType.DMA
    out, grad_fields, sums = pl.pallas_call(
        functools.partial(kernel, dims),
        out_shape=(
            jax.ShapeDtypeStruct((C, R, L), BF16),
            jax.ShapeDtypeStruct((C, R, L), BF16),
            jax.ShapeDtypeStruct((AR_ROWS, L), F32),
        ),
        in_specs=[vmem] * 8,
        out_specs=(vmem,) * 3,
        scratch_shapes=[
            pltpu.VMEM((C * R, L), F32),
            pltpu.VMEM((R, C, L), F32),
            pltpu.VMEM((R, C, L), F32),
            pltpu.VMEM((RE, C, L), BF16),
            pltpu.VMEM((RE, C, L), BF16),
            pltpu.VMEM((7, RE, C, L), F32),
            pltpu.VMEM((RE, C, L), F32),
            pltpu.VMEM((7, 3, C, L), F32),
            pltpu.VMEM((49, C, L), F32),
            pltpu.VMEM((R, C, L), F32),
            pltpu.VMEM((2, 2, C, L), BF16),
            pltpu.VMEM((2, 2, 3, C, L), BF16),
            pltpu.VMEM((2, nx, 3, C, L), BF16),
            pltpu.VMEM((2, nzc, 4, C, L), BF16),
            pltpu.VMEM((2, nzc, 4, C, L), BF16),
            pltpu.VMEM((nzc, nx * L, 2 * L), BF16),
            pltpu.VMEM((C, HID), BF16),
            pltpu.VMEM((HID, C), BF16),
            pltpu.VMEM((3, C, 2 * L), F32),
            pltpu.VMEM((3, C, 2 * L), F32),
            pltpu.VMEM((C, HID), F32),
            pltpu.VMEM((80, HID), F32),
            pltpu.VMEM((AR_ROWS, L), F32),
            pltpu.VMEM((nlat, chunk, L), F32),
            pltpu.VMEM((ng, chunk, L), F32),
            pltpu.VMEM((nz, chunk, L), F32),
            pltpu.VMEM((nlat, chunk, L), F32),
            dma((2, 8)),
            dma((2, 8)),
            dma((2, nx)),
            dma((2, nx)),
            dma((2, nzc)),
            dma((2, nzc)),
            dma((nlat,)),
            dma((nlat,)),
            dma((ng,)),
            dma((ng,)),
            dma((nz,)),
            dma((nz,)),
            dma((nlat,)),
            dma((nlat,)),
        ],
        compiler_params=pltpu.CompilerParams(
            collective_id=0, has_side_effects=True, vmem_limit_bytes=48 * 2**20
        ),
        name="block",
    )(
        fields[0],
        cotangent[0],
        ocean_mask,
        seam_partner.reshape(nlon, L),
        params,
        up_ext,
        up_weight,
        down_weight,
    )
    up = jnp.concatenate([sums[:72], sums[72:AR_DOWN]], axis=1)
    down = jnp.concatenate([sums[AR_DOWN : AR_DOWN + C], sums[AR_DOWN + C : AR_DOWN + 2 * C]], axis=1)
    last = sums[AR_DEPTH : AR_DEPTH + C]
    return (
        out[None],
        grad_fields[None],
        last[:, :49].reshape(C, 7, 7),
        last[:, 64],
        last[:, 65],
        up[:C].T,
        up[C],
        down,
        last[:, 66],
    )


def solution(mesh):
    nlon, nlat = mesh.shape["lon"], mesh.shape["lat"]
    dims = (nlon, nlat, 4 if nlon % 16 == 0 else 2)
    cells = P(None, None, "lat", "lon")
    return jax.shard_map(
        functools.partial(shards, dims),
        mesh=mesh,
        in_specs=(cells, cells, P("lat", "lon")) + (P(),) * 8,
        out_specs=(cells, cells) + (P(),) * 7,
        check_vma=False,
    )
```

time: 499 us -> 82 us (0.16)
  waiting for transfers between devices: 244 us -> 0 us
  blocking collectives: 107 us -> 0 us
  Pallas kernels: 0 us -> 72.1 us
  other arithmetic: 45.4 us -> 1.32 us
  local copies, waits for them, and re-layouts: 46.1 us -> 6.51 us
  starting transfers between devices: 24.7 us -> 0 us
  matrix products: 15.1 us -> 0 us
  between operations: 15.4 us -> 0.79 us
    psum x1 -> x0, waiting for transfers between devices: 195 us -> none  [shards(): lax.psum((g_depth, gain_gradient, g_bias, g_up_w, g_up_b, g_down, g_scale...]
    psum x1 -> x0, blocking collectives: 107 us -> none  [shards(): lax.psum((g_depth, gain_gradient, g_bias, g_up_w, g_up_b, g_down, g_scale...]
    pallas_call x0 -> x1, Pallas kernels: none -> 72.1 us  [shards(): pl.pallas_call(functools.partial(kernel, dims), out_shape=(jax.ShapeDtype...]
    all_gather x2 -> x0, waiting for transfers between devices: 42.1 us -> none  [the longest x1 42.1 us: shards(): lax.all_gather(upper, 'lon', axis=3, tiled=True)]
    ppermute x8 -> x0, starting transfers between devices: 24.6 us -> none  [the longest x4 16.4 us: extended_2(): lax.ppermute(tail, axis, [(i, (i + 1) % count) for i in range(ends)])]
    reduce_sum x7 -> x0, other arithmetic: 22.2 us -> none  [the longest x4 10.9 us: shards(): jnp.sum(d_conv_f * extended[:, :, row_tap:row_tap + rows, col_tap:col_tap...]
    dot_general x6 -> x0, matrix products: 15.1 us -> none  [the longest x1 6.9 us: cell_terms(): jnp.dot(up_weight, normalized_output, preferred_element_type=jnp.float32)]
    all_gather x2 -> x0, local copies, waits for them, and re-layouts: 12.9 us -> none  [the longest x1 6.45 us: shards(): lax.all_gather(margin.astype(jnp.bfloat16), 'lon', axis=3, tiled=True)]
  transfers between devices with their start and end apart: 11 -> 0, of which waited for: 3 -> 0; matrix products, arithmetic and copies ran while one was open for 12% -> 0% of each run, Pallas kernels for 0% -> 0%
where the time goes in v1:
time: 82 us; the launch traced here: 80.7 us
  Pallas kernels  72.1 us (88%)
  local copies, waits for them, and re-layouts  6.51 us (8%)
  other arithmetic  1.32 us (2%)
    pallas_call x1, Pallas kernels, shards(): pl.pallas_call(functools.partial(kernel, dims), out_shape=(jax.ShapeDtype...  72.1 us
    unnamed x25, local copies, waits for them, and re-layouts  4.3 us

profile of v1, /device:TPU:1, one launch (start us, length us, event | category | flops | bytes accessed | tf_op | source)
XLA Modules:
  0.0 80.7 jit_solution(8606460444530784124)
XLA Ops:
  0.6 0.0 copy-start.6
  0.7 0.1 pad.6.clone
  0.7 0.6 copy-done.6
  1.4 0.1 copy.27
  1.5 0.5 copy-done.8
  2.0 0.1 copy.28
  2.1 0.5 copy-done.9
  2.7 0.1 copy.29
  2.8 0.5 copy-done.10
  3.3 0.1 copy.30
  3.5 0.0 copy-start.7
  3.5 0.0 copy-start
  3.5 0.0 copy-start.1
  3.5 0.1 concatenate.12
  3.6 0.0 copy-done.5
  3.6 0.1 copy.31.up_ref
  3.8 0.4 copy-done.7
  4.1 0.1 broadcast_in_dim.36
  4.2 0.1 maximum_maximum_fusion.upx_ref
  4.3 0.0 copy-done.4
  4.3 0.0 copy-done.3
  4.3 0.0 copy-done.2
  4.3 0.1 copy-done
  4.4 0.1 copy-done.1
  4.5 72.1 %block.1 = (bf16[64,16,128]{2,1,0:T(8,128)(2,1)S(1)}, bf16[64,16,128]{2,1,0:T(8,128)(2,1)S(1)}, f32[384,128]{1,0:T(8,128)S(1)}) custom-call(bf16[64,16,128]{2,1,0:T(8,128)(2,1)S(1)} %bitcast.15, bf16[64,16,128]{2,1,0:T(8,128)(2,1)S(1)} %bitcast.16, s32[16,128]{1,0:T(8,128)S(1)} %copy-done.4, s32[32,128]{1,0:T(8,128)S(1)} %bitcast.19, ...), custom_call_target="tpu_custom_call" | custom-call | tf_op jit(solution)/shard_map/block/pallas_call | solution.py:600
  76.6 0.7 slice_reduce_fusion
  77.4 0.1 copy.34
  77.5 0.6 reshape.29
  78.1 0.6 pad_maximum_fusion.1
  78.7 0.7 fusion.1
  79.3 0.7 copy.37
  80.0 0.7 copy.38
  (15 shorter events, 0.1 us)
Async XLA Ops:
  0.6 0.7 copy-start.6
  1.4 0.7 copy-start.8
  1.4 2.3 %copy-start.5 = (bf16[256,64]{0,1:T(8,128)(2,1)S(1)}, bf16[256,64]{0,1:T(8,128)(2,1)}, u32[]{:S(2)}) copy-start(bf16[256,64]{0,1:T(8,128)(2,1)} %param.18) | copy-start | bytes 98308
  2.0 0.7 copy-start.9
  2.7 0.7 copy-start.10
  2.7 1.6 %copy-start.4 = (s32[16,128]{1,0:T(8,128)S(1)}, s32[16,128]{1,0:T(8,128)}, u32[]{:S(2)}) copy-start(s32[16,128]{1,0:T(8,128)} %mask_ref.1) | copy-start | bytes 24580
  3.3 1.0 %copy-start.3 = (s32[4096]{0:T(1024)S(1)}, s32[4096]{0:T(1024)}, u32[]{:S(2)}) copy-start(s32[4096]{0:T(1024)} %param.14) | copy-start | bytes 49156
  3.4 0.9 %copy-start.2 = (bf16[64,256]{1,0:T(8,128)(2,1)S(1)}, bf16[64,256]{1,0:T(8,128)(2,1)}, u32[]{:S(2)}) copy-start(bf16[64,256]{1,0:T(8,128)(2,1)} %down_ref.1) | copy-start | bytes 98308
  3.5 0.7 copy-start.7
  3.5 1.0 %copy-start = (bf16[1,64,16,128]{3,2,1,0:T(8,128)(2,1)S(1)}, bf16[1,64,16,128]{3,2,1,0:T(8,128)(2,1)}, u32[]{:S(2)}) copy-start(bf16[1,64,16,128]{3,2,1,0:T(8,128)(2,1)} %param.11) | copy-start | bytes 786436
  3.5 1.0 %copy-start.1 = (bf16[1,64,16,128]{3,2,1,0:T(8,128)(2,1)S(1)}, bf16[1,64,16,128]{3,2,1,0:T(8,128)(2,1)}, u32[]{:S(2)}) copy-start(bf16[1,64,16,128]{3,2,1,0:T(8,128)(2,1)} %param.12) | copy-start | bytes 786436

commit v2 on v1

v2 whole, which is shorter than its diff:
```python
import functools
import math

import jax
import jax.numpy as jnp
from jax import lax
from jax.experimental import pallas as pl
from jax.experimental.pallas import tpu as pltpu
from jax.sharding import PartitionSpec as P

F32 = jnp.float32
BF16 = jnp.bfloat16
MESH = pl.DeviceIdType.MESH
C = 64
R = 16
L = 128
HID = 256
RE = R + 6
BLOCK = 4
WIDE = BLOCK * L
MLP_ROWS = 256
REST_ROWS = 32
CORES = 2

ERF_P = 0.3275911 / math.sqrt(2.0)
ERF_C = (
    0.5 * 0.254829592,
    0.5 * -0.284496736,
    0.5 * 1.421413741,
    0.5 * -1.453152027,
    0.5 * 1.061405429,
)
PDF = 1.0 / math.sqrt(2.0 * math.pi)


def phi_and_density(v):
    d = 1.0 + ERF_P * jnp.abs(v)
    t = pl.reciprocal(d, approx=True)
    t = t * (2.0 - d * t)
    e = jnp.exp(-0.5 * (v * v))
    poly = ERF_C[4]
    for coef in ERF_C[3::-1]:
        poly = poly * t + coef
    tail = poly * t * e
    return jnp.where(v >= 0.0, 1.0 - tail, tail), e


def nt_dot(a, b):
    return lax.dot_general(a, b, (((1,), (1,)), ((), ())), preferred_element_type=F32)


def dot(a, b):
    return jnp.dot(a, b, preferred_element_type=F32)


def roll(x, amount):
    amount %= L
    return pltpu.roll(x, amount, x.ndim - 1) if amount else x


class PartSum:
    def __init__(self, at, src, bufs, sems, owners):
        self.at, self.src, self.owners = at, src, owners
        self.b1, self.b2, self.b3, self.out = bufs
        self.sems = sems
        self.chunk = self.b1.shape[1]

    def piece(self, p):
        return self.src.at[pl.ds(pl.multiple_of(p * self.chunk, 8), self.chunk)]

    def others(self, count, body):
        @pl.loop(0, count)
        def _(p):
            @pl.when(p != self.at.lat)
            def _():
                body(p)

    def owner(self, body):
        if self.owners == self.at.nlat:
            body()
        else:
            pl.when(self.at.lat < self.owners)(body)

    def first(self, to, slot):
        return remote(self.piece(to), self.b1.at[slot], self.sems[0].at[to], self.sems[1].at[slot],
                      self.at.place(self.at.lon, to))

    def second(self, j, mine):
        at = self.at
        to = (at.mg + j) % at.ng
        slot = at.mg if mine else to
        return remote(self.b2.at[at.mg], self.b2.at[slot], self.sems[2].at[to], self.sems[3].at[slot],
                      at.place(at.lon_of_group(to), at.lat))

    def third(self, j, mine):
        at = self.at
        to = (at.mz + j) % at.nz
        slot = at.mz if mine else to
        return remote(self.b3.at[at.mz], self.b3.at[slot], self.sems[4].at[to], self.sems[5].at[slot],
                      at.place(at.mx * at.nzc + to * CORES + at.mc, at.lat))

    def last(self, to, slot):
        return remote(self.out.at[self.at.lat % self.owners], self.out.at[slot], self.sems[6].at[to],
                      self.sems[7].at[slot], self.at.place(self.at.lon, to))

    def step1(self):
        self.others(self.owners, lambda p: self.first(p, self.at.lat).start())

    def step2(self):
        at = self.at

        def go():
            self.others(at.nlat, lambda p: self.first(0, p).wait_recv())
            self.b1[at.lat] = self.src[pl.ds(pl.multiple_of(at.lat * self.chunk, 8), self.chunk)]
            self.b2[at.mg] = jnp.sum(self.b1[...], axis=0)

            @pl.loop(1, at.ng)
            def _(j):
                self.second(j, True).start()

        self.owner(go)

    def step3(self):
        at = self.at

        def go():
            @pl.loop(1, at.ng)
            def _(j):
                self.second(j, False).wait()

            self.b3[at.mz] = jnp.sum(self.b2[...], axis=0)

            @pl.loop(1, at.nz)
            def _(j):
                self.third(j, True).start()

        self.owner(go)

    def step4(self):
        at = self.at

        def go():
            @pl.loop(1, at.nz)
            def _(j):
                self.third(j, False).wait()

            self.out[at.lat] = jnp.sum(self.b3[...], axis=0)
            self.others(at.nlat, lambda p: self.last(p, at.lat).start())

        self.owner(go)

    def finish(self):
        at = self.at
        self.others(self.owners, lambda p: self.last(p, p).wait_recv())
        self.owner(lambda: self.others(at.nlat, lambda p: self.last(p, at.lat).wait_send()))
        self.others(self.owners, lambda p: self.first(p, at.lat).wait_send())


def remote(src, dst, send, recv, where):
    return pltpu.make_async_remote_copy(
        src_ref=src, dst_ref=dst, send_sem=send, recv_sem=recv,
        device_id=where, device_id_type=MESH,
    )


class Place:
    def __init__(self, dims):
        nlon, nlat, nx = dims
        self.nlon, self.nlat, self.nx = dims
        self.nzc = nlon // nx
        self.nz = self.nzc // CORES
        self.ng = nx * CORES
        self.lon = lax.axis_index("lon")
        self.lat = lax.axis_index("lat")
        self.mx, self.mzc = self.lon // self.nzc, self.lon % self.nzc
        self.mz, self.mc = self.mzc // CORES, self.mzc % CORES
        self.mg = self.mx * CORES + self.mc

    def place(self, a, b):
        return {"lon": a, "lat": b}

    def lon_of_group(self, g):
        return (g // CORES) * self.nzc + self.mz * CORES + g % CORES


def kernel(
    dims,
    fields_hbm,
    cot_hbm,
    mask_hbm,
    seam_hbm,
    depth_hbm,
    gain_hbm,
    bias_hbm,
    scale_hbm,
    upt_hbm,
    upb_hbm,
    down_hbm,
    out_ref,
    gf_ref,
    mlp_ref,
    rest_ref,
    rows_f,
    gmask,
    outr,
    xf,
    df,
    shifts,
    hal,
    fshift,
    wts,
    conv,
    edges,
    edgesr,
    pks,
    pkr,
    fx,
    fzs,
    fzr,
    onehot,
    pmat,
    upx,
    downt,
    parb,
    acc_s,
    acc_down,
    acc_up,
    mlp_src,
    rest_src,
    mlp1,
    mlp2,
    mlp3,
    mlpg,
    rest1,
    rest2,
    rest3,
    restg,
    halo_send,
    halo_recv,
    fx_send,
    fx_recv,
    fz_send,
    fz_recv,
    in_sems,
    fields_ref,
    cot_ref,
    mask_ref,
    seam_ref,
    depth_ref,
    gain_ref,
    bias_ref,
    scale_ref,
    upt_ref,
    upb_ref,
    down_ref,
    *part_sems,
):
    at = Place(dims)
    nlon, nlat, nx, nzc, ng = at.nlon, at.nlat, at.nx, at.nzc, at.ng
    lon, lat, mx, mzc, mg = at.lon, at.lat, at.mx, at.mzc, at.mg
    place = at.place
    left, right = (lon + nlon - 1) % nlon, (lon + 1) % nlon
    down_lat, up_lat = (lat + nlat - 1) % nlat, (lat + 1) % nlat
    lats = (down_lat, lat, up_lat)
    is_top = lat == nlat - 1
    is_bottom = lat == 0
    mlp_sum = PartSum(at, mlp_src, (mlp1, mlp2, mlp3, mlpg), part_sems[:8], nlat)
    rest_sum = PartSum(at, rest_src, (rest1, rest2, rest3, restg), part_sems[8:], restg.shape[0])

    barrier = pltpu.get_barrier_semaphore()

    def hail(a, b):
        pl.semaphore_signal(barrier, inc=1, device_id=place(a, b), device_id_type=MESH)

    for b in lats:
        hail(left, b)
        hail(right, b)
    hail(lon, down_lat)
    hail(lon, up_lat)

    @pl.loop(1, nlat)
    def _(j):
        hail(lon, (lat + j) % nlat)

    @pl.loop(1, ng)
    def _(j):
        hail(at.lon_of_group((mg + j) % ng), lat)

    @pl.loop(1, nzc)
    def _(j):
        hail(mx * nzc + (mzc + j) % nzc, lat)

    loads = [
        pltpu.make_async_copy(src, dst, in_sems.at[n])
        for n, (src, dst) in enumerate(
            (
                (fields_hbm, fields_ref),
                (cot_hbm, cot_ref),
                (mask_hbm, mask_ref),
                (seam_hbm, seam_ref),
                (depth_hbm, depth_ref),
                (gain_hbm, gain_ref),
                (bias_hbm, bias_ref),
                (scale_hbm, scale_ref),
                (upt_hbm, upt_ref),
                (upb_hbm, upb_ref),
                (down_hbm, down_ref),
            )
        )
    ]
    for load in loads:
        load.start()

    lane = lax.broadcasted_iota(jnp.int32, (C, L), 1)
    slot_of_lane = lane // 8
    low_half = lane < 64

    def row_copies(ph):
        return [
            remote(edges.at[ph, 0], edgesr.at[ph, 1],
                   halo_send.at[ph, 0], halo_recv.at[ph, 0], place(lon, down_lat)),
            remote(edges.at[ph, 1], edgesr.at[ph, 0],
                   halo_send.at[ph, 1], halo_recv.at[ph, 1], place(lon, up_lat)),
        ]

    def pack_copies(ph, kinds, src):
        return [
            remote(pks.at[src, side], pkr.at[ph, side, k],
                   halo_send.at[ph, 2 + 3 * side + k], halo_recv.at[ph, 2 + 3 * side + k], place(to, lats[k]))
            for side, to in ((0, left), (1, right))
            for k in kinds
        ]

    def pack(src, row, which):
        low = jnp.zeros((C, L), F32)
        high = jnp.zeros((C, L), F32)
        for i in which:
            here = slot_of_lane == i
            low = jnp.where(here, roll(row(i), 8 * i), low)
            high = jnp.where(here, roll(row(i), 8 * i + 8), high)
        pks[src, 0] = low.astype(BF16)
        pks[src, 1] = high.astype(BF16)

    def unpack(ph, rows):
        for k, ext_rows, first in ((2, range(0, 3), 13), (1, range(3, R + 3), -3), (0, range(R + 3, RE), -R - 3)):
            from_right = pkr[ph, 0, k].astype(F32)
            from_left = pkr[ph, 1, k].astype(F32)
            for u in ext_rows:
                i = u + first
                hal[u] = jnp.where(low_half, roll(from_right, -8 * i), roll(from_left, 120 - 8 * i))
        rows[0:3] = edgesr[ph, 0].astype(F32)
        rows[R + 3 : RE] = edgesr[ph, 1].astype(F32)

    def shifted(q, main, halo, lanes):
        if q == 3:
            return main
        edge = lanes >= 125 + q if q < 3 else lanes < q - 3
        return roll(jnp.where(edge, halo, main), 3 - q)

    def part_of(s):
        return pl.ds(pl.multiple_of(s * 8, 8), 8)

    def fold_copy(ph, j, mine):
        to = (mx + j) % nx
        slot = mx if mine else to
        return remote(edges.at[ph, 1], fx.at[ph, slot], fx_send.at[ph, to], fx_recv.at[ph, slot],
                      place(to * nzc + mzc, lat))

    def fold_copy2(ph, j, mine):
        t = (mzc + j) % nzc
        slot = mzc if mine else t
        return remote(fzs.at[ph, t], fzr.at[ph, slot], fz_send.at[ph, t], fz_recv.at[ph, slot],
                      place(mx * nzc + t, lat))

    def fold_first(ph):
        fx[ph, mx] = edges[ph, 1]

        @pl.loop(1, nx)
        def _(j):
            fold_copy(ph, j, True).start()

    def fold_second(ph):
        @pl.loop(1, nx)
        def _(j):
            fold_copy(ph, j, False).wait()

        held = jnp.concatenate([fx[ph, x].reshape(3 * C, L) for x in range(nx)], axis=1)

        @pl.loop(0, nzc)
        def _(t):
            got = dot(held, onehot[t])
            mirrored = [got[C * (2 - k) : C * (3 - k)] for k in range(3)]
            slot = slot_of_lane % 8
            ends = mirrored[2][:, L:]
            for k in (1, 0):
                ends = jnp.where(slot == k, mirrored[k][:, L:], ends)
            for k in range(3):
                fzs[ph, t, k] = mirrored[k][:, :L].astype(BF16)
            fzs[ph, t, 3] = ends.astype(BF16)

        fzr[ph, mzc] = fzs[ph, mzc]

        @pl.loop(1, nzc)
        def _(j):
            fold_copy2(ph, j, True).start()

    def fold_last(ph):
        @pl.loop(1, nzc)
        def _(j):
            fold_copy2(ph, j, False).wait()

        total = fzr[ph, 0].astype(F32)
        for t in range(1, nzc):
            total = total + fzr[ph, t].astype(F32)
        halos = [
            jnp.where(low_half, roll(total[3], -8 * k), roll(total[3], 56 - 8 * k))
            for k in range(3)
        ]
        return [total[k] for k in range(3)], halos

    loads[0].wait()
    rows_f[...] = fields_ref[...].astype(F32).reshape(C * R, L)
    for i in range(R):
        xf[3 + i] = rows_f[pl.ds(i, C, stride=R), :]
    edges[0, 0] = xf[3:6].astype(BF16)
    edges[0, 1] = xf[R : R + 3].astype(BF16)
    pack(0, lambda i: xf[3 + i], range(R))
    pl.semaphore_wait(barrier, 8 + (nlat - 1) + (ng - 1) + (nzc - 1))
    sent = row_copies(0) + pack_copies(0, (0, 1, 2), 0)
    for copy in sent:
        copy.start()
    for load in loads[1:]:
        load.wait()

    @pl.when(is_top)
    def _():
        fold_first(0)
        partner = seam_ref[0:1, 0:1]
        rows_i = lax.broadcasted_iota(jnp.int32, (nx * L, 2 * L), 0)
        held_col = L * ((rows_i // L) * nzc + mzc) + rows_i % L
        col = lax.broadcasted_iota(jnp.int32, (1, 2 * L), 1)
        packed = col - L
        ahead = jnp.where(packed < 64, L + packed % 8, packed % 8 - 8)
        offset = jnp.where(col < L, col, ahead)

        @pl.loop(0, nzc)
        def _(t):
            wanted = (partner - L * (mx * nzc + t) - offset) & (nlon * L - 1)
            onehot[t] = jnp.where(held_col == wanted, 1.0, 0.0).astype(BF16)

    def eye(n):
        return jnp.where(
            lax.broadcasted_iota(jnp.int32, (n, n), 0) == lax.broadcasted_iota(jnp.int32, (n, n), 1), 1.0, 0.0
        ).astype(BF16)

    pmat[...] = jnp.zeros_like(pmat)
    for a in range(7):
        pmat[8 * a : 8 * a + 7] = depth_ref[a].astype(F32)
    for n, ref in enumerate((gain_ref, bias_ref, scale_ref)):
        pmat[56 + n : 57 + n] = ref[...].astype(F32)
    par = nt_dot(eye(C), pmat[...].astype(BF16))
    for a in range(7):
        for q in range(7):
            wts[a * 7 + q] = jnp.broadcast_to(par[:, 8 * a + q : 8 * a + q + 1], (C, L))
    for n in range(3):
        parb[n] = jnp.broadcast_to(par[:, 56 + n : 57 + n], (C, WIDE))
    first_row = lax.broadcasted_iota(jnp.int32, (16, HID), 0) == 0
    upb = upb_ref[...].astype(F32)
    upb = jnp.concatenate([upb[0:1], upb[1:2]], axis=1)
    bias_row = jnp.where(first_row, jnp.broadcast_to(upb, (16, HID)), 0.0)
    with_bias = jnp.concatenate([upt_ref[...], bias_row.astype(BF16)], axis=0)
    upx[...] = nt_dot(eye(HID), with_bias).astype(BF16)
    downt[...] = nt_dot(eye(HID), down_ref[...]).astype(BF16)
    acc_s[...] = jnp.zeros_like(acc_s)
    acc_down[...] = jnp.zeros_like(acc_down)
    acc_up[...] = jnp.zeros_like(acc_up)
    rows_f[...] = cot_ref[...].astype(F32).reshape(C * R, L)
    for i in range(R):
        gmask[i] = rows_f[pl.ds(i, C, stride=R), :] * mask_ref[i : i + 1, :].astype(F32)

    @pl.when(is_top)
    def _():
        fold_second(0)

    for copy in sent:
        copy.wait()
    unpack(0, xf)

    @pl.when(is_bottom)
    def _():
        for u in range(3):
            xf[u] = jnp.zeros((C, L), F32)
            hal[u] = jnp.zeros((C, L), F32)

    @pl.when(is_top)
    def _():
        mains, halos = fold_last(0)
        for k in range(3):
            xf[R + 3 + k] = mains[k]
            hal[R + 3 + k] = halos[k]

    @pl.loop(0, C // 8)
    def _(s):
        cs = part_of(s)
        lanes = lax.broadcasted_iota(jnp.int32, (RE, 8, L), 2)
        total = jnp.zeros((R, 8, L), F32)
        for q in range(7):
            ext = shifted(q, xf[:, cs, :], hal[:, cs, :], lanes)
            shifts[q, :, cs, :] = ext
            for a in range(7):
                total = total + wts[a * 7 + q, cs, :][None] * ext[a : a + R]
        conv[:, cs, :] = total

    def flat(x):
        return jnp.concatenate([x[i] for i in range(BLOCK)], axis=1)

    @pl.loop(0, R // BLOCK)
    def _(step):
        first = BLOCK * ((3 * step) % (R // BLOCK))
        rows = pl.ds(first, BLOCK)
        gain, bias, scale = parb[0], parb[1], parb[2]
        x = flat(conv[rows])
        mean = jnp.mean(x, axis=0, keepdims=True)
        x = x - mean
        rstd = lax.rsqrt(jnp.mean(x * x, axis=0, keepdims=True) + 1e-06)
        xhat = x * rstd
        normed = (xhat * gain + bias).astype(BF16)
        normed_one = jnp.concatenate([normed, jnp.ones((16, WIDE), BF16)], axis=0)
        pre = dot(upx[...], normed_one)
        phi, density = phi_and_density(pre)
        hidden = (pre * phi).astype(BF16)
        slope = phi + pre * density * PDF
        branch = dot(down_ref[...], hidden)
        mask = mask_ref[rows, :].astype(F32)
        mask = jnp.concatenate([mask[i : i + 1] for i in range(BLOCK)], axis=1)
        out = mask * (flat(xf[pl.ds(3 + first, BLOCK)]) + scale * branch)
        g = flat(gmask[rows])
        d_branch = (g * scale).astype(BF16)
        acc_s[2] += g * branch
        acc_down[...] += nt_dot(d_branch, hidden)
        d_hidden = dot(downt[...], d_branch)
        d_pre = (d_hidden * slope).astype(BF16)
        acc_up[...] += nt_dot(normed_one, d_pre)
        d_normed = dot(upt_ref[...], d_pre)
        acc_s[0] += d_normed * xhat
        acc_s[1] += d_normed
        gd = d_normed * gain
        d_conv = rstd * (
            gd
            - jnp.mean(gd, axis=0, keepdims=True)
            - xhat * jnp.mean(gd * xhat, axis=0, keepdims=True)
        )
        d_conv = d_conv.astype(BF16).astype(F32)
        for i in range(BLOCK):
            outr[first + i] = out[:, L * i : L * (i + 1)]
            df[3 + first + i] = d_conv[:, L * i : L * (i + 1)]

        @pl.when(step == 1)
        def _():
            edges[1, 0] = df[3:6].astype(BF16)
            edges[1, 1] = df[R : R + 3].astype(BF16)
            pack(1, lambda i: df[3 + i], (0, 1, 2, 13, 14, 15))
            for copy in row_copies(1) + pack_copies(1, (0, 2), 1):
                copy.start()

            @pl.when(is_top)
            def _():
                fold_first(1)

    pack(2, lambda i: df[3 + i], range(R))
    for copy in pack_copies(1, (1,), 2):
        copy.start()

    up = acc_up[...]
    mlp_src[0:64] = up[:64, :L]
    mlp_src[64:128] = up[:64, L:]
    down = acc_down[...]
    mlp_src[128:192] = down[:, :L]
    mlp_src[192:256] = down[:, L:]
    mlp_sum.step1()

    @pl.when(is_top)
    def _():
        fold_second(1)

    @pl.loop(0, C // 8)
    def _(s):
        cs = part_of(s)
        d_conv = df[3 : R + 3, cs, :]
        lanes = lax.broadcasted_iota(jnp.int32, (8, L), 1)
        got = jnp.zeros((8, L), F32)
        for q in range(7):
            ext = shifts[q, :, cs, :]
            for a in range(7):
                tap = jnp.sum(d_conv * ext[a : a + R], axis=0)
                got = jnp.where(lanes == a * 8 + q, jnp.sum(tap, axis=1, keepdims=True), got)
        for n in range(3):
            got = jnp.where(lanes == 56 + n, jnp.sum(acc_s[n, cs, :], axis=1, keepdims=True), got)
        rows_f[cs, :] = got

    rows_f[C : 2 * C] = jnp.zeros((C, L), F32)
    taps = jnp.transpose(rows_f[0:L, :])[:C]
    up_b = up[C : C + 1]
    row_of = lax.broadcasted_iota(jnp.int32, (C, L), 0)
    for k in range(4):
        piece = jnp.broadcast_to(up_b[:, L * (k // 2) : L * (k // 2) + L], (C, L))
        taps = jnp.where(row_of == 59 + k, roll(piece, 64 * (k % 2)), taps)
    rest_src[...] = jnp.where(low_half[:32], taps[:32], roll(taps[32:], 64))
    rest_sum.step1()
    mlp_sum.step2()

    for copy in row_copies(1) + pack_copies(1, (0, 2), 1) + pack_copies(1, (1,), 2):
        copy.wait()
    unpack(1, df)

    def clear(u):
        df[u] = jnp.zeros((C, L), F32)
        hal[u] = jnp.zeros((C, L), F32)

    @pl.when(is_bottom)
    def _():
        for u in range(3):
            clear(u)

    @pl.when(is_top)
    def _():
        for u in range(R + 3, RE):
            clear(u)

    def adjoint(first, last):
        @pl.loop(first, last)
        def _(s):
            cs = part_of(s)
            lanes = lax.broadcasted_iota(jnp.int32, (RE, 8, L), 2)
            total = gmask[:, cs, :]
            for q in range(7):
                ext = shifted(6 - q, df[:, cs, :], hal[:, cs, :], lanes)
                for a in range(7):
                    total = total + wts[a * 7 + q, cs, :][None] * ext[6 - a : 6 - a + R]
            gmask[:, cs, :] = total

    adjoint(0, C // 16)
    rest_sum.step2()
    mlp_sum.step3()
    adjoint(C // 16, C // 8)
    rest_sum.step3()
    mlp_sum.step4()

    @pl.when(is_top)
    def _():
        mains, halos = fold_last(1)
        for k in range(3):
            for q in range(7):
                fshift[q, k] = shifted(q, mains[k], halos[k], lane)
        for k in range(3):
            total = gmask[R - 1 - k]
            for a in range(k + 4, 7):
                for q in range(7):
                    total = total + wts[a * 7 + q] * fshift[q, a - k - 4]
            gmask[R - 1 - k] = total

    for i in range(R):
        rows_f[pl.ds(i, C, stride=R), :] = gmask[i]
    gf_ref[...] = rows_f[...].reshape(C, R, L).astype(BF16)
    rest_sum.step4()
    for i in range(R):
        rows_f[pl.ds(i, C, stride=R), :] = outr[i]
    out_ref[...] = rows_f[...].reshape(C, R, L).astype(BF16)
    mlp_sum.finish()
    for p in range(nlat):
        mlp_ref[p * mlp_sum.chunk : (p + 1) * mlp_sum.chunk] = mlpg[p]
    rest_sum.finish()
    for p in range(restg.shape[0]):
        rest_ref[p * rest_sum.chunk : (p + 1) * rest_sum.chunk] = restg[p]


def unpack_sums(out_ref, gf_ref, mlp_ref, rest_ref, o_out, o_gf, o_depth, o_gain, o_bias, o_up, o_upb, o_down, o_scale, sems):
    stores = [pltpu.make_async_copy(out_ref, o_out, sems.at[0]), pltpu.make_async_copy(gf_ref, o_gf, sems.at[1])]
    for store in stores:
        store.start()
    o_up[:, :L] = mlp_ref[0:64]
    o_up[:, L:] = mlp_ref[64:128]
    o_down[:, :L] = mlp_ref[128:192]
    o_down[:, L:] = mlp_ref[192:256]
    low = rest_ref[...]
    high = pltpu.roll(low, 64, 1)
    for a in range(7):
        part = low[8 * a : 8 * a + 7] if a < 4 else high[8 * a - 32 : 8 * a - 25]
        o_depth[a] = part[:, :C]
    o_gain[...] = high[24:25, :C]
    o_bias[...] = high[25:26, :C]
    o_scale[...] = high[26:27, :C]
    lane = lax.broadcasted_iota(jnp.int32, (1, L), 1)
    for k in range(2):
        o_upb[:, L * k : L * (k + 1)] = jnp.where(lane < 64, high[27 + 2 * k : 28 + 2 * k], low[28 + 2 * k : 29 + 2 * k])
    for store in stores:
        store.wait()


def shards(
    dims,
    fields,
    cotangent,
    ocean_mask,
    seam_partner,
    depth_weight,
    norm_gain,
    layer_norm_bias,
    up_weight,
    up_bias,
    down_weight,
    layer_scale,
):
    nlon, nlat, nx = dims
    nzc = nlon // nx
    nz = nzc // CORES
    ng = nx * CORES
    owners = min(4, nlat)
    vmem = pl.BlockSpec(memory_space=pltpu.VMEM)
    hbm = pl.BlockSpec(memory_space=pltpu.HBM)
    dma = pltpu.SemaphoreType.DMA

    def part_bufs(rows, n):
        chunk = rows // n
        return [pltpu.VMEM((count, chunk, L), F32) for count in (nlat, ng, nz, n)]

    def part_sems(n):
        return [dma((count,)) for count in (n, nlat, ng, ng, nz, nz, nlat, n)]

    cells = jax.ShapeDtypeStruct((C, R, L), BF16)
    out, grad_fields, mlp, rest = pl.pallas_call(
        functools.partial(kernel, dims),
        out_shape=(
            pltpu.VMEM((C, R, L), BF16),
            pltpu.VMEM((C, R, L), BF16),
            pltpu.VMEM((MLP_ROWS, L), F32),
            pltpu.VMEM((REST_ROWS, L), F32),
        ),
        in_specs=[hbm] * 11,
        out_specs=(vmem,) * 4,
        scratch_shapes=[
            pltpu.VMEM((C * R, L), F32),
            pltpu.VMEM((R, C, L), F32),
            pltpu.VMEM((R, C, L), F32),
            pltpu.VMEM((RE, C, L), F32),
            pltpu.VMEM((RE, C, L), F32),
            pltpu.VMEM((7, RE, C, L), F32),
            pltpu.VMEM((RE, C, L), F32),
            pltpu.VMEM((7, 3, C, L), F32),
            pltpu.VMEM((49, C, L), F32),
            pltpu.VMEM((R, C, L), F32),
            pltpu.VMEM((2, 2, 3, C, L), BF16),
            pltpu.VMEM((2, 2, 3, C, L), BF16),
            pltpu.VMEM((3, 2, C, L), BF16),
            pltpu.VMEM((2, 2, 3, C, L), BF16),
            pltpu.VMEM((2, nx, 3, C, L), BF16),
            pltpu.VMEM((2, nzc, 4, C, L), BF16),
            pltpu.VMEM((2, nzc, 4, C, L), BF16),
            pltpu.VMEM((nzc, nx * L, 2 * L), BF16),
            pltpu.VMEM((C, C), F32),
            pltpu.VMEM((HID, 80), BF16),
            pltpu.VMEM((HID, C), BF16),
            pltpu.VMEM((3, C, WIDE), F32),
            pltpu.VMEM((3, C, WIDE), F32),
            pltpu.VMEM((C, HID), F32),
            pltpu.VMEM((80, HID), F32),
            pltpu.VMEM((MLP_ROWS, L), F32),
            pltpu.VMEM((REST_ROWS, L), F32),
            *part_bufs(MLP_ROWS, nlat),
            *part_bufs(REST_ROWS, owners),
            dma((2, 8)),
            dma((2, 8)),
            dma((2, nx)),
            dma((2, nx)),
            dma((2, nzc)),
            dma((2, nzc)),
            dma((11,)),
            pltpu.VMEM((C, R, L), BF16),
            pltpu.VMEM((C, R, L), BF16),
            pltpu.VMEM((R, L), jnp.int32),
            pltpu.VMEM((nlon, L), jnp.int32),
            pltpu.VMEM((7, 7, C), BF16),
            pltpu.VMEM((1, C), BF16),
            pltpu.VMEM((1, C), BF16),
            pltpu.VMEM((1, C), BF16),
            pltpu.VMEM((C, HID), BF16),
            pltpu.VMEM((2, L), BF16),
            pltpu.VMEM((C, HID), BF16),
            *part_sems(nlat),
            *part_sems(owners),
        ],
        compiler_params=pltpu.CompilerParams(
            collective_id=0, has_side_effects=True, vmem_limit_bytes=60 * 2**20
        ),
        name="block",
    )(
        fields[0],
        cotangent[0],
        ocean_mask,
        seam_partner.reshape(nlon, L),
        jnp.transpose(depth_weight, (1, 2, 0)),
        norm_gain[None],
        layer_norm_bias[None],
        layer_scale[None],
        up_weight.T,
        up_bias.reshape(2, L),
        down_weight,
    )
    vector = jax.ShapeDtypeStruct((1, C), F32)
    wide = jax.ShapeDtypeStruct((C, HID), F32)
    out, grad_fields, depth, gain, bias, up, up_b, down, scale = pl.pallas_call(
        unpack_sums,
        out_shape=(
            cells,
            cells,
            jax.ShapeDtypeStruct((7, 7, C), F32),
            vector,
            vector,
            wide,
            jax.ShapeDtypeStruct((1, HID), F32),
            wide,
            vector,
        ),
        in_specs=[vmem] * 4,
        out_specs=(hbm,) * 2 + (vmem,) * 7,
        name="unpack_sums",
        scratch_shapes=[dma((2,))],
    )(*(pltpu.with_memory_space_constraint(x, pltpu.VMEM) for x in (out, grad_fields, mlp, rest)))
    return (
        out[None],
        grad_fields[None],
        jnp.transpose(depth, (2, 0, 1)),
        gain[0],
        bias[0],
        up.T,
        up_b[0],
        down,
        scale[0],
    )


def solution(mesh):
    nlon, nlat = mesh.shape["lon"], mesh.shape["lat"]
    dims = (nlon, nlat, 4 if nlon % 16 == 0 else 2)
    cells = P(None, None, "lat", "lon")
    return jax.shard_map(
        functools.partial(shards, dims),
        mesh=mesh,
        in_specs=(cells, cells, P("lat", "lon")) + (P(),) * 8,
        out_specs=(cells, cells) + (P(),) * 7,
        check_vma=False,
    )
```

time: 82 us -> 66.2 us (0.81); the launches traced: 80.7 us -> 66.1 us
  Pallas kernels: 72.1 us -> 65.4 us
  local copies, waits for them, and re-layouts: 6.51 us -> 0 us
  other arithmetic: 1.32 us -> 0 us
    pallas_call x1 -> x2, Pallas kernels: 72.1 us -> 65.4 us  [the longest x1 64 us: shards(): pl.pallas_call(functools.partial(kernel, dims), out_shape=(pltpu.VMEM((C,...]
    unnamed x25 -> x0, local copies, waits for them, and re-layouts: 4.3 us -> none
    slice x5 -> x0, local copies, waits for them, and re-layouts: 0.84 us -> none  [the longest x1 0.74 us: shards(): last[:, 66]]
where the time goes in v2:
time: 66.2 us; the launch traced here: 66.1 us
  Pallas kernels  65.4 us (99%)
    pallas_call x1, Pallas kernels, shards(): pl.pallas_call(functools.partial(kernel, dims), out_shape=(pltpu.VMEM((C,...  64 us
    pallas_call x1, Pallas kernels, shards(): pl.pallas_call(unpack_sums, out_shape=(cells, cells, jax.ShapeDtypeStruct...  1.47 us

profile of v2, /device:TPU:1, one launch (start us, length us, event | category | flops | bytes accessed | tf_op | source)
XLA Modules:
  0.0 66.1 jit_solution(528664906673631226)
XLA Ops:
  0.6 64.0 %block.1 = (bf16[64,16,128]{2,1,0:T(8,128)(2,1)S(1)}, bf16[64,16,128]{2,1,0:T(8,128)(2,1)S(1)}, f32[256,128]{1,0:T(8,128)S(1)}, f32[32,128]{1,0:T(8,128)S(1)}) custom-call(bf16[64,16,128]{2,1,0:T(8,128)(2,1)} %bitcast.17, bf16[64,16,128]{2,1,0:T(8,128)(2,1)} %bitcast.18, s32[16,128]{1,0:T(8,128)} %mask_hbm.1, s32[32,128]{1,0:T(8,128)} %bitcast.20, ...), custom_call_target="tpu_custom_call" | custom-call | tf_op jit(solution)/shard_map/block/pallas_call | solution.py:731
  64.6 1.5 %unpack_sums.1 = (bf16[64,16,128]{2,1,0:T(8,128)(2,1)}, bf16[64,16,128]{2,1,0:T(8,128)(2,1)}, f32[7,7,64]{2,1,0:T(8,128)}, f32[1,64]{1,0:T(1,128)}, f32[1,64]{1,...) custom-call(bf16[64,16,128]{2,1,0:T(8,128)(2,1)S(1)} %get-tuple-element.22.out_ref, ...), custom_call_target="tpu_custom_call" | custom-call | tf_op jit(solution)/shard_map/unpack_sums/pallas_call | solution.py:811

commit v3 on v2

--- a/solution.py
+++ b/solution.py
@@ -363,7 +363,7 @@
     def fold_copy(ph, j, mine):
         to = (mx + j) % nx
         slot = mx if mine else to
-        return remote(edges.at[ph, 1], fx.at[ph, slot], fx_send.at[ph, to], fx_recv.at[ph, slot],
+        return remote(fx.at[ph, mx], fx.at[ph, slot], fx_send.at[ph, to], fx_recv.at[ph, slot],
                       place(to * nzc + mzc, lat))
 
     def fold_copy2(ph, j, mine):
@@ -372,8 +372,8 @@
         return remote(fzs.at[ph, t], fzr.at[ph, slot], fz_send.at[ph, t], fz_recv.at[ph, slot],
                       place(mx * nzc + t, lat))
 
-    def fold_first(ph):
-        fx[ph, mx] = edges[ph, 1]
+    def fold_first(ph, rows):
+        fx[ph, mx] = rows[R : R + 3].astype(BF16)
 
         @pl.loop(1, nx)
         def _(j):
@@ -434,7 +434,7 @@
 
     @pl.when(is_top)
     def _():
-        fold_first(0)
+        fold_first(0, xf)
         partner = seam_ref[0:1, 0:1]
         rows_i = lax.broadcasted_iota(jnp.int32, (nx * L, 2 * L), 0)
         held_col = L * ((rows_i // L) * nzc + mzc) + rows_i % L
@@ -492,31 +492,42 @@
             xf[u] = jnp.zeros((C, L), F32)
             hal[u] = jnp.zeros((C, L), F32)
 
-    @pl.when(is_top)
-    def _():
-        mains, halos = fold_last(0)
-        for k in range(3):
-            xf[R + 3 + k] = mains[k]
-            hal[R + 3 + k] = halos[k]
-
-    @pl.loop(0, C // 8)
-    def _(s):
-        cs = part_of(s)
-        lanes = lax.broadcasted_iota(jnp.int32, (RE, 8, L), 2)
-        total = jnp.zeros((R, 8, L), F32)
-        for q in range(7):
-            ext = shifted(q, xf[:, cs, :], hal[:, cs, :], lanes)
-            shifts[q, :, cs, :] = ext
-            for a in range(7):
-                total = total + wts[a * 7 + q, cs, :][None] * ext[a : a + R]
-        conv[:, cs, :] = total
+    def conv_rows(first, count):
+        ext_rows = pl.ds(first, count + 6)
+
+        @pl.loop(0, C // 8)
+        def _(s):
+            cs = part_of(s)
+            lanes = lax.broadcasted_iota(jnp.int32, (count + 6, 8, L), 2)
+            total = jnp.zeros((count, 8, L), F32)
+            for q in range(7):
+                ext = shifted(q, xf[ext_rows, cs, :], hal[ext_rows, cs, :], lanes)
+                shifts[q, ext_rows, cs, :] = ext
+                for a in range(7):
+                    total = total + wts[a * 7 + q, cs, :][None] * ext[a : a + count]
+            conv[pl.ds(first, count), cs, :] = total
+
+    conv_rows(0, R - BLOCK)
+    top_flag = (lat + 1) // nlat
 
     def flat(x):
         return jnp.concatenate([x[i] for i in range(BLOCK)], axis=1)
 
     @pl.loop(0, R // BLOCK)
     def _(step):
-        first = BLOCK * ((3 * step) % (R // BLOCK))
+        first = BLOCK * (((3 - 2 * top_flag) * step) % (R // BLOCK))
+
+        @pl.when(step == 3 * top_flag)
+        def _():
+            @pl.when(is_top)
+            def _():
+                mains, halos = fold_last(0)
+                for k in range(3):
+                    xf[R + 3 + k] = mains[k]
+                    hal[R + 3 + k] = halos[k]
+
+            conv_rows(R - BLOCK, BLOCK)
+
         rows = pl.ds(first, BLOCK)
         gain, bias, scale = parb[0], parb[1], parb[2]
         x = flat(conv[rows])
@@ -563,9 +574,9 @@
             for copy in row_copies(1) + pack_copies(1, (0, 2), 1):
                 copy.start()
 
-            @pl.when(is_top)
-            def _():
-                fold_first(1)
+    @pl.when(is_top)
+    def _():
+        fold_first(1, df)
 
     pack(2, lambda i: df[3 + i], range(R))
     for copy in pack_copies(1, (1,), 2):
@@ -578,10 +589,6 @@
     mlp_src[128:192] = down[:, :L]
     mlp_src[192:256] = down[:, L:]
     mlp_sum.step1()
-
-    @pl.when(is_top)
-    def _():
-        fold_second(1)
 
     @pl.loop(0, C // 8)
     def _(s):
@@ -607,6 +614,11 @@
         taps = jnp.where(row_of == 59 + k, roll(piece, 64 * (k % 2)), taps)
     rest_src[...] = jnp.where(low_half[:32], taps[:32], roll(taps[32:], 64))
     rest_sum.step1()
+
+    @pl.when(is_top)
+    def _():
+        fold_second(1)
+
     mlp_sum.step2()
 
     for copy in row_copies(1) + pack_copies(1, (0, 2), 1) + pack_copies(1, (1,), 2):

time: 66.2 us -> 63.6 us (0.961)
  Pallas kernels: 65.4 us -> 62.8 us
    pallas_call x1, Pallas kernels: 64 us -> 61.3 us  [shards(): pl.pallas_call(functools.partial(kernel, dims), out_shape=(pltpu.VMEM((C,...]
where the time goes in v3:
time: 63.6 us; the launch traced here: 63.4 us
  Pallas kernels  62.8 us (99%)
  between operations  0.65 us (1%)
    pallas_call x1, Pallas kernels, shards(): pl.pallas_call(functools.partial(kernel, dims), out_shape=(pltpu.VMEM((C,...  61.3 us
    pallas_call x1, Pallas kernels, shards(): pl.pallas_call(unpack_sums, out_shape=(cells, cells, jax.ShapeDtypeStruct...  1.47 us

profile of v3, /device:TPU:1, one launch (start us, length us, event | category | flops | bytes accessed | tf_op | source)
XLA Modules:
  0.0 63.4 jit_solution(10664064351233930513)
XLA Ops:
  0.6 61.3 %block.1 = (bf16[64,16,128]{2,1,0:T(8,128)(2,1)S(1)}, bf16[64,16,128]{2,1,0:T(8,128)(2,1)S(1)}, f32[256,128]{1,0:T(8,128)S(1)}, f32[32,128]{1,0:T(8,128)S(1)}) custom-call(bf16[64,16,128]{2,1,0:T(8,128)(2,1)} %bitcast.17, bf16[64,16,128]{2,1,0:T(8,128)(2,1)} %bitcast.18, s32[16,128]{1,0:T(8,128)} %mask_hbm.1, s32[32,128]{1,0:T(8,128)} %bitcast.20, ...), custom_call_target="tpu_custom_call" | custom-call | tf_op jit(solution)/shard_map/block/pallas_call | solution.py:743
  61.9 1.5 %unpack_sums.1 = (bf16[64,16,128]{2,1,0:T(8,128)(2,1)}, bf16[64,16,128]{2,1,0:T(8,128)(2,1)}, f32[7,7,64]{2,1,0:T(8,128)}, f32[1,64]{1,0:T(1,128)}, f32[1,64]{1,...) custom-call(bf16[64,16,128]{2,1,0:T(8,128)(2,1)S(1)} %get-tuple-element.22.out_ref, ...), custom_call_target="tpu_custom_call" | custom-call | tf_op jit(solution)/shard_map/unpack_sums/pallas_call | solution.py:823

commit v4 on v3

--- a/solution.py
+++ b/solution.py
@@ -215,8 +215,10 @@
     pks,
     pkr,
     fx,
-    fzs,
-    fzr,
+    fsel,
+    fz,
+    fout,
+    fin,
     onehot,
     pmat,
     upx,
@@ -241,6 +243,8 @@
     fx_recv,
     fz_send,
     fz_recv,
+    fc_send,
+    fc_recv,
     in_sems,
     fields_ref,
     cot_ref,
@@ -258,6 +262,7 @@
     at = Place(dims)
     nlon, nlat, nx, nzc, ng = at.nlon, at.nlat, at.nx, at.nzc, at.ng
     lon, lat, mx, mzc, mg = at.lon, at.lat, at.mx, at.mzc, at.mg
+    nz, mz, mc = at.nz, at.mz, at.mc
     place = at.place
     left, right = (lon + nlon - 1) % nlon, (lon + 1) % nlon
     down_lat, up_lat = (lat + nlat - 1) % nlat, (lat + 1) % nlat
@@ -286,9 +291,9 @@
     def _(j):
         hail(at.lon_of_group((mg + j) % ng), lat)
 
-    @pl.loop(1, nzc)
+    @pl.loop(1, nz)
     def _(j):
-        hail(mx * nzc + (mzc + j) % nzc, lat)
+        hail(mx * nzc + (mz + j) % nz * CORES + mc, lat)
 
     loads = [
         pltpu.make_async_copy(src, dst, in_sems.at[n])
@@ -367,10 +372,20 @@
                       place(to * nzc + mzc, lat))
 
     def fold_copy2(ph, j, mine):
-        t = (mzc + j) % nzc
-        slot = mzc if mine else t
-        return remote(fzs.at[ph, t], fzr.at[ph, slot], fz_send.at[ph, t], fz_recv.at[ph, slot],
-                      place(mx * nzc + t, lat))
+        to = (mz + j) % nz
+        slot = mz if mine else to
+        return remote(fsel.at[ph, to], fz.at[ph, slot], fz_send.at[ph, to], fz_recv.at[ph, slot],
+                      place(mx * nzc + to * CORES + mc, lat))
+
+    def fold_copy3(ph):
+        return remote(fout.at[ph, 1], fin.at[ph], fc_send.at[ph], fc_recv.at[ph],
+                      place(mx * nzc + mz * CORES + 1 - mc, lat))
+
+    def needed(x, m, z):
+        start = L * (x * nzc + m)
+        least = seam_ref[0:1, 0:1] - L * (mx * nzc + z * CORES) - (CORES * L + 2)
+        last = nlon * L - 1
+        return (((start - least) & last) < CORES * L + 6) | (((least - start) & last) < L)
 
     def fold_first(ph, rows):
         fx[ph, mx] = rows[R : R + 3].astype(BF16)
@@ -384,34 +399,41 @@
         def _(j):
             fold_copy(ph, j, False).wait()
 
-        held = jnp.concatenate([fx[ph, x].reshape(3 * C, L) for x in range(nx)], axis=1)
-
-        @pl.loop(0, nzc)
-        def _(t):
-            got = dot(held, onehot[t])
+        @pl.loop(0, nz)
+        def _(z):
+            picked = jnp.zeros((3, C, L), F32)
+            for x in range(nx):
+                use = jnp.where(needed(x, mzc, z), 1.0, 0.0)
+                picked = jnp.where(jnp.broadcast_to(use, (C, L))[None] > 0.5, fx[ph, x].astype(F32), picked)
+            fsel[ph, z] = picked.astype(BF16)
+
+        fz[ph, mz] = fsel[ph, mz]
+
+        @pl.loop(1, nz)
+        def _(j):
+            fold_copy2(ph, j, True).start()
+
+    def fold_third(ph):
+        @pl.loop(1, nz)
+        def _(j):
+            fold_copy2(ph, j, False).wait()
+
+        held = jnp.concatenate([fz[ph, z].reshape(3 * C, L) for z in range(nz)], axis=1)
+        for other in range(CORES):
+            got = dot(held, onehot[other])
             mirrored = [got[C * (2 - k) : C * (3 - k)] for k in range(3)]
             slot = slot_of_lane % 8
             ends = mirrored[2][:, L:]
             for k in (1, 0):
                 ends = jnp.where(slot == k, mirrored[k][:, L:], ends)
             for k in range(3):
-                fzs[ph, t, k] = mirrored[k][:, :L].astype(BF16)
-            fzs[ph, t, 3] = ends.astype(BF16)
-
-        fzr[ph, mzc] = fzs[ph, mzc]
-
-        @pl.loop(1, nzc)
-        def _(j):
-            fold_copy2(ph, j, True).start()
+                fout[ph, other, k] = mirrored[k][:, :L].astype(BF16)
+            fout[ph, other, 3] = ends.astype(BF16)
+        fold_copy3(ph).start()
 
     def fold_last(ph):
-        @pl.loop(1, nzc)
-        def _(j):
-            fold_copy2(ph, j, False).wait()
-
-        total = fzr[ph, 0].astype(F32)
-        for t in range(1, nzc):
-            total = total + fzr[ph, t].astype(F32)
+        fold_copy3(ph).wait()
+        total = fout[ph, 0].astype(F32) + fin[ph].astype(F32)
         halos = [
             jnp.where(low_half, roll(total[3], -8 * k), roll(total[3], 56 - 8 * k))
             for k in range(3)
@@ -425,28 +447,34 @@
     edges[0, 0] = xf[3:6].astype(BF16)
     edges[0, 1] = xf[R : R + 3].astype(BF16)
     pack(0, lambda i: xf[3 + i], range(R))
-    pl.semaphore_wait(barrier, 8 + (nlat - 1) + (ng - 1) + (nzc - 1))
+    pl.semaphore_wait(barrier, 8 + (nlat - 1) + (ng - 1) + (nz - 1))
     sent = row_copies(0) + pack_copies(0, (0, 1, 2), 0)
     for copy in sent:
         copy.start()
-    for load in loads[1:]:
-        load.wait()
+    loads[3].wait()
 
     @pl.when(is_top)
     def _():
         fold_first(0, xf)
-        partner = seam_ref[0:1, 0:1]
-        rows_i = lax.broadcasted_iota(jnp.int32, (nx * L, 2 * L), 0)
-        held_col = L * ((rows_i // L) * nzc + mzc) + rows_i % L
-        col = lax.broadcasted_iota(jnp.int32, (1, 2 * L), 1)
-        packed = col - L
-        ahead = jnp.where(packed < 64, L + packed % 8, packed % 8 - 8)
-        offset = jnp.where(col < L, col, ahead)
-
-        @pl.loop(0, nzc)
-        def _(t):
-            wanted = (partner - L * (mx * nzc + t) - offset) & (nlon * L - 1)
-            onehot[t] = jnp.where(held_col == wanted, 1.0, 0.0).astype(BF16)
+        rows_i = lax.broadcasted_iota(jnp.int32, (nz * L, L), 0)
+        block = jnp.full((nz * L, L), -(2**20), jnp.int32)
+        for z in range(nz):
+            for x in range(nx):
+                here = jnp.where(needed(x, z * CORES + mc, mz), 1, 0)
+                here = (jnp.broadcast_to(here, (nz * L, L)) > 0) & (rows_i // L == z)
+                block = jnp.where(here, L * (x * nzc + z * CORES + mc), block)
+        held_col = block + rows_i % L
+        col = lax.broadcasted_iota(jnp.int32, (1, L), 1)
+        ahead = jnp.where(col < 64, L + col % 8, col % 8 - 8)
+        for other in range(CORES):
+            core = mc + other * (1 - 2 * mc)
+            origin = seam_ref[0:1, 0:1] - L * (mx * nzc + mz * CORES + core)
+            for half, offset in enumerate((col, ahead)):
+                wanted = (origin - offset) & (nlon * L - 1)
+                onehot[other, :, L * half : L * (half + 1)] = jnp.where(held_col == wanted, 1.0, 0.0).astype(BF16)
+
+    for load in loads[1:3] + loads[4:]:
+        load.wait()
 
     def eye(n):
         return jnp.where(
@@ -508,6 +536,11 @@
             conv[pl.ds(first, count), cs, :] = total
 
     conv_rows(0, R - BLOCK)
+
+    @pl.when(is_top)
+    def _():
+        fold_third(0)
+
     top_flag = (lat + 1) // nlat
 
     def flat(x):
@@ -652,6 +685,11 @@
             gmask[:, cs, :] = total
 
     adjoint(0, C // 16)
+
+    @pl.when(is_top)
+    def _():
+        fold_third(1)
+
     rest_sum.step2()
     mlp_sum.step3()
     adjoint(C // 16, C // 8)
@@ -766,9 +804,11 @@
             pltpu.VMEM((3, 2, C, L), BF16),
             pltpu.VMEM((2, 2, 3, C, L), BF16),
             pltpu.VMEM((2, nx, 3, C, L), BF16),
-            pltpu.VMEM((2, nzc, 4, C, L), BF16),
-            pltpu.VMEM((2, nzc, 4, C, L), BF16),
-            pltpu.VMEM((nzc, nx * L, 2 * L), BF16),
+            pltpu.VMEM((2, nz, 3, C, L), BF16),
+            pltpu.VMEM((2, nz, 3, C, L), BF16),
+            pltpu.VMEM((2, CORES, 4, C, L), BF16),
+            pltpu.VMEM((2, 4, C, L), BF16),
+            pltpu.VMEM((CORES, nz * L, 2 * L), BF16),
             pltpu.VMEM((C, C), F32),
             pltpu.VMEM((HID, 80), BF16),
             pltpu.VMEM((HID, C), BF16),
@@ -784,8 +824,10 @@
             dma((2, 8)),
             dma((2, nx)),
             dma((2, nx)),
-            dma((2, nzc)),
-            dma((2, nzc)),
+            dma((2, nz)),
+            dma((2, nz)),
+            dma((2,)),
+            dma((2,)),
             dma((11,)),
             pltpu.VMEM((C, R, L), BF16),
             pltpu.VMEM((C, R, L), BF16),

time: 63.6 us -> 53.5 us (0.84); the launches traced: 63.4 us -> 52.5 us
  Pallas kernels: 62.8 us -> 51.9 us
    pallas_call x1, Pallas kernels: 61.3 us -> 50.4 us  [shards(): pl.pallas_call(functools.partial(kernel, dims), out_shape=(pltpu.VMEM((C,...]
where the time goes in v4:
time: 53.5 us; the launch traced here: 52.5 us
  Pallas kernels  51.9 us (97%)
  between operations  0.65 us (1%)
    pallas_call x1, Pallas kernels, shards(): pl.pallas_call(functools.partial(kernel, dims), out_shape=(pltpu.VMEM((C,...  50.4 us
    pallas_call x1, Pallas kernels, shards(): pl.pallas_call(unpack_sums, out_shape=(cells, cells, jax.ShapeDtypeStruct...  1.47 us

profile of v4, /device:TPU:1, one launch (start us, length us, event | category | flops | bytes accessed | tf_op | source)
XLA Modules:
  0.0 52.5 jit_solution(18411567382706456916)
XLA Ops:
  0.6 50.4 %block.1 = (bf16[64,16,128]{2,1,0:T(8,128)(2,1)S(1)}, bf16[64,16,128]{2,1,0:T(8,128)(2,1)S(1)}, f32[256,128]{1,0:T(8,128)S(1)}, f32[32,128]{1,0:T(8,128)S(1)}) custom-call(bf16[64,16,128]{2,1,0:T(8,128)(2,1)} %bitcast.17, bf16[64,16,128]{2,1,0:T(8,128)(2,1)} %bitcast.18, s32[16,128]{1,0:T(8,128)} %mask_hbm.1, s32[32,128]{1,0:T(8,128)} %bitcast.20, ...), custom_call_target="tpu_custom_call" | custom-call | tf_op jit(solution)/shard_map/block/pallas_call | solution.py:781
  51.0 1.5 %unpack_sums.1 = (bf16[64,16,128]{2,1,0:T(8,128)(2,1)}, bf16[64,16,128]{2,1,0:T(8,128)(2,1)}, f32[7,7,64]{2,1,0:T(8,128)}, f32[1,64]{1,0:T(1,128)}, f32[1,64]{1,...) custom-call(bf16[64,16,128]{2,1,0:T(8,128)(2,1)S(1)} %get-tuple-element.22.out_ref, ...), custom_call_target="tpu_custom_call" | custom-call | tf_op jit(solution)/shard_map/unpack_sums/pallas_call | solution.py:865

commit v5 on v4

--- a/solution.py
+++ b/solution.py
@@ -346,13 +346,19 @@
         pks[src, 0] = low.astype(BF16)
         pks[src, 1] = high.astype(BF16)
 
-    def unpack(ph, rows):
-        for k, ext_rows, first in ((2, range(0, 3), 13), (1, range(3, R + 3), -3), (0, range(R + 3, RE), -R - 3)):
-            from_right = pkr[ph, 0, k].astype(F32)
-            from_left = pkr[ph, 1, k].astype(F32)
-            for u in ext_rows:
-                i = u + first
-                hal[u] = jnp.where(low_half, roll(from_right, -8 * i), roll(from_left, 120 - 8 * i))
+    def unpack(ph, k, ext_rows):
+        from_right = pkr[ph, 0, k].astype(F32)
+        from_left = pkr[ph, 1, k].astype(F32)
+        for u in ext_rows:
+            i = (u - 3) % R
+            hal[u] = jnp.where(low_half, roll(from_right, -8 * i), roll(from_left, 120 - 8 * i))
+
+    def unpack_beside(ph):
+        unpack(ph, 1, range(3, R + 3))
+
+    def unpack_rows(ph, rows):
+        unpack(ph, 2, range(0, 3))
+        unpack(ph, 0, range(R + 3, RE))
         rows[0:3] = edgesr[ph, 0].astype(F32)
         rows[R + 3 : RE] = edgesr[ph, 1].astype(F32)
 
@@ -448,8 +454,9 @@
     edges[0, 1] = xf[R : R + 3].astype(BF16)
     pack(0, lambda i: xf[3 + i], range(R))
     pl.semaphore_wait(barrier, 8 + (nlat - 1) + (ng - 1) + (nz - 1))
-    sent = row_copies(0) + pack_copies(0, (0, 1, 2), 0)
-    for copy in sent:
+    beside = pack_copies(0, (1,), 0)
+    sent = row_copies(0) + pack_copies(0, (0, 2), 0)
+    for copy in beside + sent:
         copy.start()
     loads[3].wait()
 
@@ -506,20 +513,6 @@
     for i in range(R):
         gmask[i] = rows_f[pl.ds(i, C, stride=R), :] * mask_ref[i : i + 1, :].astype(F32)
 
-    @pl.when(is_top)
-    def _():
-        fold_second(0)
-
-    for copy in sent:
-        copy.wait()
-    unpack(0, xf)
-
-    @pl.when(is_bottom)
-    def _():
-        for u in range(3):
-            xf[u] = jnp.zeros((C, L), F32)
-            hal[u] = jnp.zeros((C, L), F32)
-
     def conv_rows(first, count):
         ext_rows = pl.ds(first, count + 6)
 
@@ -535,11 +528,26 @@
                     total = total + wts[a * 7 + q, cs, :][None] * ext[a : a + count]
             conv[pl.ds(first, count), cs, :] = total
 
-    conv_rows(0, R - BLOCK)
+    for copy in beside:
+        copy.wait()
+    unpack_beside(0)
+    conv_rows(3, R - 6)
 
     @pl.when(is_top)
     def _():
-        fold_third(0)
+        fold_second(0)
+
+    for copy in sent:
+        copy.wait()
+    unpack_rows(0, xf)
+
+    @pl.when(is_bottom)
+    def _():
+        for u in range(3):
+            xf[u] = jnp.zeros((C, L), F32)
+            hal[u] = jnp.zeros((C, L), F32)
+
+    conv_rows(0, 3)
 
     top_flag = (lat + 1) // nlat
 
@@ -559,7 +567,7 @@
                     xf[R + 3 + k] = mains[k]
                     hal[R + 3 + k] = halos[k]
 
-            conv_rows(R - BLOCK, BLOCK)
+            conv_rows(R - 3, 3)
 
         rows = pl.ds(first, BLOCK)
         gain, bias, scale = parb[0], parb[1], parb[2]
@@ -607,6 +615,10 @@
             for copy in row_copies(1) + pack_copies(1, (0, 2), 1):
                 copy.start()
 
+            @pl.when(is_top)
+            def _():
+                fold_third(0)
+
     @pl.when(is_top)
     def _():
         fold_first(1, df)
@@ -656,7 +668,8 @@
 
     for copy in row_copies(1) + pack_copies(1, (0, 2), 1) + pack_copies(1, (1,), 2):
         copy.wait()
-    unpack(1, df)
+    unpack_beside(1)
+    unpack_rows(1, df)
 
     def clear(u):
         df[u] = jnp.zeros((C, L), F32)

time: 53.5 us -> 54.8 us (1.024)
  the two profiles are of different devices: /device:TPU:1 before, /device:TPU:8 now
where the time goes in v5:
time: 54.8 us; the launch traced here: 54.7 us
  Pallas kernels  54 us (99%)
  between operations  0.65 us (1%)
    pallas_call x1, Pallas kernels, shards(): pl.pallas_call(functools.partial(kernel, dims), out_shape=(pltpu.VMEM((C,...  52.5 us
    pallas_call x1, Pallas kernels, shards(): pl.pallas_call(unpack_sums, out_shape=(cells, cells, jax.ShapeDtypeStruct...  1.47 us

profile of v5, /device:TPU:8, one launch (start us, length us, event | category | flops | bytes accessed | tf_op | source)
XLA Modules:
  0.0 54.7 jit_solution(8557861526532082544)
XLA Ops:
  0.6 52.5 %block.1 = (bf16[64,16,128]{2,1,0:T(8,128)(2,1)S(1)}, bf16[64,16,128]{2,1,0:T(8,128)(2,1)S(1)}, f32[256,128]{1,0:T(8,128)S(1)}, f32[32,128]{1,0:T(8,128)S(1)}) custom-call(bf16[64,16,128]{2,1,0:T(8,128)(2,1)} %bitcast.17, bf16[64,16,128]{2,1,0:T(8,128)(2,1)} %bitcast.18, s32[16,128]{1,0:T(8,128)} %mask_hbm.1, s32[32,128]{1,0:T(8,128)} %bitcast.20, ...), custom_call_target="tpu_custom_call" | custom-call | tf_op jit(solution)/shard_map/block/pallas_call | solution.py:794
  53.2 1.5 %unpack_sums.1 = (bf16[64,16,128]{2,1,0:T(8,128)(2,1)}, bf16[64,16,128]{2,1,0:T(8,128)(2,1)}, f32[7,7,64]{2,1,0:T(8,128)}, f32[1,64]{1,0:T(1,128)}, f32[1,64]{1,...) custom-call(bf16[64,16,128]{2,1,0:T(8,128)(2,1)S(1)} %get-tuple-element.22.out_ref, ...), custom_call_target="tpu_custom_call" | custom-call | tf_op jit(solution)/shard_map/unpack_sums/pallas_call | solution.py:878

commit v6 on v5

--- a/solution.py
+++ b/solution.py
@@ -454,6 +454,10 @@
     edges[0, 1] = xf[R : R + 3].astype(BF16)
     pack(0, lambda i: xf[3 + i], range(R))
     pl.semaphore_wait(barrier, 8 + (nlat - 1) + (ng - 1) + (nz - 1))
+    @pl.when(is_top)
+    def _():
+        fold_first(0, xf)
+
     beside = pack_copies(0, (1,), 0)
     sent = row_copies(0) + pack_copies(0, (0, 2), 0)
     for copy in beside + sent:
@@ -462,7 +466,6 @@
 
     @pl.when(is_top)
     def _():
-        fold_first(0, xf)
         rows_i = lax.broadcasted_iota(jnp.int32, (nz * L, L), 0)
         block = jnp.full((nz * L, L), -(2**20), jnp.int32)
         for z in range(nz):
@@ -531,11 +534,11 @@
     for copy in beside:
         copy.wait()
     unpack_beside(0)
-    conv_rows(3, R - 6)
-
     @pl.when(is_top)
     def _():
         fold_second(0)
+
+    conv_rows(3, R - 6)
 
     for copy in sent:
         copy.wait()

time: 54.8 us -> 53.6 us (0.978)
  Pallas kernels: 54 us -> 52.8 us
    pallas_call x1, Pallas kernels: 52.5 us -> 51.3 us  [shards(): pl.pallas_call(functools.partial(kernel, dims), out_shape=(pltpu.VMEM((C,...]
where the time goes in v6:
time: 53.6 us; the launch traced here: 53.5 us
  Pallas kernels  52.8 us (99%)
  between operations  0.65 us (1%)
    pallas_call x1, Pallas kernels, shards(): pl.pallas_call(functools.partial(kernel, dims), out_shape=(pltpu.VMEM((C,...  51.3 us
    pallas_call x1, Pallas kernels, shards(): pl.pallas_call(unpack_sums, out_shape=(cells, cells, jax.ShapeDtypeStruct...  1.47 us

profile of v6, /device:TPU:8, one launch (start us, length us, event | category | flops | bytes accessed | tf_op | source)
XLA Modules:
  0.0 53.5 jit_solution(13152890771238402508)
XLA Ops:
  0.6 51.3 %block.1 = (bf16[64,16,128]{2,1,0:T(8,128)(2,1)S(1)}, bf16[64,16,128]{2,1,0:T(8,128)(2,1)S(1)}, f32[256,128]{1,0:T(8,128)S(1)}, f32[32,128]{1,0:T(8,128)S(1)}) custom-call(bf16[64,16,128]{2,1,0:T(8,128)(2,1)} %bitcast.17, bf16[64,16,128]{2,1,0:T(8,128)(2,1)} %bitcast.18, s32[16,128]{1,0:T(8,128)} %mask_hbm.1, s32[32,128]{1,0:T(8,128)} %bitcast.20, ...), custom_call_target="tpu_custom_call" | custom-call | tf_op jit(solution)/shard_map/block/pallas_call | solution.py:797
  52.0 1.5 %unpack_sums.1 = (bf16[64,16,128]{2,1,0:T(8,128)(2,1)}, bf16[64,16,128]{2,1,0:T(8,128)(2,1)}, f32[7,7,64]{2,1,0:T(8,128)}, f32[1,64]{1,0:T(1,128)}, f32[1,64]{1,...) custom-call(bf16[64,16,128]{2,1,0:T(8,128)(2,1)S(1)} %get-tuple-element.22.out_ref, ...), custom_call_target="tpu_custom_call" | custom-call | tf_op jit(solution)/shard_map/unpack_sums/pallas_call | solution.py:881

commit v7 on v6

--- a/solution.py
+++ b/solution.py
@@ -31,13 +31,14 @@
     0.5 * 1.061405429,
 )
 PDF = 1.0 / math.sqrt(2.0 * math.pi)
+HALF_LOG2E = -0.5 * math.log2(math.e)
 
 
 def phi_and_density(v):
     d = 1.0 + ERF_P * jnp.abs(v)
     t = pl.reciprocal(d, approx=True)
     t = t * (2.0 - d * t)
-    e = jnp.exp(-0.5 * (v * v))
+    e = jnp.exp2(HALF_LOG2E * (v * v))
     poly = ERF_C[4]
     for coef in ERF_C[3::-1]:
         poly = poly * t + coef
@@ -272,29 +273,6 @@
     mlp_sum = PartSum(at, mlp_src, (mlp1, mlp2, mlp3, mlpg), part_sems[:8], nlat)
     rest_sum = PartSum(at, rest_src, (rest1, rest2, rest3, restg), part_sems[8:], restg.shape[0])
 
-    barrier = pltpu.get_barrier_semaphore()
-
-    def hail(a, b):
-        pl.semaphore_signal(barrier, inc=1, device_id=place(a, b), device_id_type=MESH)
-
-    for b in lats:
-        hail(left, b)
-        hail(right, b)
-    hail(lon, down_lat)
-    hail(lon, up_lat)
-
-    @pl.loop(1, nlat)
-    def _(j):
-        hail(lon, (lat + j) % nlat)
-
-    @pl.loop(1, ng)
-    def _(j):
-        hail(at.lon_of_group((mg + j) % ng), lat)
-
-    @pl.loop(1, nz)
-    def _(j):
-        hail(mx * nzc + (mz + j) % nz * CORES + mc, lat)
-
     loads = [
         pltpu.make_async_copy(src, dst, in_sems.at[n])
         for n, (src, dst) in enumerate(
@@ -315,6 +293,29 @@
     ]
     for load in loads:
         load.start()
+
+    barrier = pltpu.get_barrier_semaphore()
+
+    def hail(a, b):
+        pl.semaphore_signal(barrier, inc=1, device_id=place(a, b), device_id_type=MESH)
+
+    for b in lats:
+        hail(left, b)
+        hail(right, b)
+    hail(lon, down_lat)
+    hail(lon, up_lat)
+
+    @pl.loop(1, nlat)
+    def _(j):
+        hail(lon, (lat + j) % nlat)
+
+    @pl.loop(1, ng)
+    def _(j):
+        hail(at.lon_of_group((mg + j) % ng), lat)
+
+    @pl.loop(1, nz)
+    def _(j):
+        hail(mx * nzc + (mz + j) % nz * CORES + mc, lat)
 
     lane = lax.broadcasted_iota(jnp.int32, (C, L), 1)
     slot_of_lane = lane // 8

time: 53.6 us -> 53.6 us (level)
  no operation moved by 1% of the time
where the time goes in v7:
time: 53.6 us; the launch traced here: 53.5 us
  Pallas kernels  52.8 us (99%)
  between operations  0.65 us (1%)
    pallas_call x1, Pallas kernels, shards(): pl.pallas_call(functools.partial(kernel, dims), out_shape=(pltpu.VMEM((C,...  51.3 us
    pallas_call x1, Pallas kernels, shards(): pl.pallas_call(unpack_sums, out_shape=(cells, cells, jax.ShapeDtypeStruct...  1.47 us

profile of v7, /device:TPU:8, one launch (start us, length us, event | category | flops | bytes accessed | tf_op | source)
XLA Modules:
  0.0 53.5 jit_solution(13921254992107315316)
XLA Ops:
  0.6 51.3 %block.1 = (bf16[64,16,128]{2,1,0:T(8,128)(2,1)S(1)}, bf16[64,16,128]{2,1,0:T(8,128)(2,1)S(1)}, f32[256,128]{1,0:T(8,128)S(1)}, f32[32,128]{1,0:T(8,128)S(1)}) custom-call(bf16[64,16,128]{2,1,0:T(8,128)(2,1)} %bitcast.17, bf16[64,16,128]{2,1,0:T(8,128)(2,1)} %bitcast.18, s32[16,128]{1,0:T(8,128)} %mask_hbm.1, s32[32,128]{1,0:T(8,128)} %bitcast.20, ...), custom_call_target="tpu_custom_call" | custom-call | tf_op jit(solution)/shard_map/block/pallas_call | solution.py:798
  52.0 1.5 %unpack_sums.1 = (bf16[64,16,128]{2,1,0:T(8,128)(2,1)}, bf16[64,16,128]{2,1,0:T(8,128)(2,1)}, f32[7,7,64]{2,1,0:T(8,128)}, f32[1,64]{1,0:T(1,128)}, f32[1,64]{1,...) custom-call(bf16[64,16,128]{2,1,0:T(8,128)(2,1)S(1)} %get-tuple-element.22.out_ref, ...), custom_call_target="tpu_custom_call" | custom-call | tf_op jit(solution)/shard_map/unpack_sums/pallas_call | solution.py:882
